TPU v7x, 512 devices: a whole 4x8x8 slice. The times are simulated.
512 devices in a mesh: pair: 8 (over x, core), role: 2 (over z_lo), shard: 32 (over z_hi, y).
Axes of the slice: x: 4, y: 8, z: 8 (z_hi: 4, z_lo: 2; z = z_hi * 2 + z_lo), core: 2. Of those that a mesh axis runs over, the one named last changes fastest.
Arguments:
- queries: bfloat16 [3072, 64, 128], P(('pair', 'role', 'shard')), parts along dimension 0, may hold values from -100 to 100
- cache_keys: bfloat16 [3072, 128, 512], P(('pair', 'role', 'shard')), parts along dimension 0, may hold values from -4 to 4
- cache_values: bfloat16 [3072, 128, 512], P(('pair', 'role', 'shard')), parts along dimension 0, may hold values from -6 to 6
- new_keys: bfloat16 [3072, 512], P(('pair', 'role', 'shard')), parts along dimension 0, may hold values from -6 to 6
- new_values: bfloat16 [3072, 512], P(('pair', 'role', 'shard')), parts along dimension 0, may hold values from -6 to 6
- lengths: int32 [3072], P(('pair', 'role', 'shard')), parts along dimension 0, may hold values from 1 to 128, 24576 in all
- residual: bfloat16 [3072, 8192], P(('pair', 'role', 'shard')), parts along dimension 0, may hold values from -6 to 6
- norm_gain: float32 [8192], replicated, may hold values from 0.1 to 1.9
- gate_weight: bfloat16 [8192, 4096], P('role', 'shard'), may hold values from -0.0625 to 0.0625
- up_weight: bfloat16 [8192, 4096], P('role', 'shard'), may hold values from -0.0625 to 0.0625
- down_weight: bfloat16 [4096, 8192], P('shard', 'role'), may hold values from -0.09375 to 0.09375
Outputs:
- layer_out: bfloat16 [3072, 8192], P(('pair', 'role', 'shard')), parts along dimension 0
There are 8 independent parts, one for each index of `pair`. A program takes and returns all parts, laid end to end along the dimension named above; an argument that names none is the same for every part. Nothing has to cross between parts.
Inputs may be any that keep to these rules, and one draw needn't show every extreme that they name: `lengths`: some request has all 128 slots valid.
All inputs are finite; a program needn't handle non-finite values. No bound on the sum of `lengths` on one device may be relied on, other than what follows from the above.
Results may differ from a plain program's by a relative error of at most 0.02.
Values may be sent and summed in bfloat16 or wider, within the bound.
A program may use at most 64 MiB of HBM per device.

v0:
```python
import jax
import jax.numpy as jnp
from jax import lax
from jax.sharding import PartitionSpec as P

HD = 128
QH = 64
KVH = 4


def attention_rows(queries, cache_keys, cache_values, new_keys, new_values, lengths):
    count = queries.shape[0]
    slots = cache_keys.shape[1]
    groups = QH // KVH
    grouped = queries.reshape(count, KVH, groups, HD)
    keys_four = cache_keys.reshape(count, slots, KVH, HD)
    values_four = cache_values.reshape(count, slots, KVH, HD)
    new_key_three = new_keys.reshape(count, KVH, HD)
    new_value_three = new_values.reshape(count, KVH, HD)
    scale = 1.0 / jnp.sqrt(jnp.float32(HD))
    scores = (
        jnp.einsum("rkgd,rlkd->rkgl", grouped, keys_four, preferred_element_type=jnp.float32)
        * scale
    )
    own = (
        jnp.einsum("rkgd,rkd->rkg", grouped, new_key_three, preferred_element_type=jnp.float32)
        * scale
    )
    valid = jnp.arange(slots)[None, :] < lengths[:, None]
    valid = valid[:, None, None, :]
    scores = jnp.where(valid, scores, jnp.float32(-1e30))
    top = jnp.maximum(jnp.max(scores, axis=-1), own)
    weights = jnp.where(valid, jnp.exp(scores - top[..., None]), jnp.float32(0.0))
    own_weight = jnp.exp(own - top)
    total = jnp.sum(weights, axis=-1) + own_weight
    summed = jnp.einsum(
        "rkgl,rlkd->rkgd",
        weights.astype(jnp.bfloat16),
        values_four,
        preferred_element_type=jnp.float32,
    )
    own_low = own_weight.astype(jnp.bfloat16).astype(jnp.float32)
    summed = summed + own_low[..., None] * new_value_three[:, :, None, :].astype(jnp.float32)
    return (summed / total[..., None]).reshape(count, QH * HD)


def feed_rows(normed, norm_weights):
    gate_weight, up_weight, down_weight = norm_weights
    width = gate_weight.shape[1]
    halves = lax.all_to_all(normed, "role", split_axis=1, concat_axis=0, tiled=True)
    piece = lax.all_gather(halves, "shard", axis=0, tiled=True)
    gate_part = jnp.dot(piece, gate_weight, preferred_element_type=jnp.float32)
    up_part = jnp.dot(piece, up_weight, preferred_element_type=jnp.float32)
    both = jnp.concatenate([gate_part, up_part], axis=1)
    both = lax.psum(both.astype(jnp.bfloat16), "role").astype(jnp.float32)
    hidden = (jax.nn.silu(both[:, :width]) * both[:, width:]).astype(jnp.bfloat16)
    mine = lax.psum_scatter(
        jnp.dot(hidden, down_weight, preferred_element_type=jnp.float32).astype(jnp.bfloat16),
        "shard",
        scatter_dimension=0,
        tiled=True,
    ).astype(jnp.float32)
    return lax.all_to_all(
        mine.astype(jnp.bfloat16), "role", split_axis=0, concat_axis=1, tiled=True
    ).astype(mine.dtype)


def per_device(
    queries,
    cache_keys,
    cache_values,
    new_keys,
    new_values,
    lengths,
    residual,
    norm_gain,
    gate_weight,
    up_weight,
    down_weight,
):
    attended = attention_rows(queries, cache_keys, cache_values, new_keys, new_values, lengths)
    mixed = residual.astype(jnp.float32) + attended
    scale = lax.rsqrt(jnp.mean(mixed * mixed, axis=-1, keepdims=True) + 1e-05)
    normed = (mixed * scale * norm_gain[None, :]).astype(jnp.bfloat16)
    weights = (gate_weight, up_weight, down_weight)
    feed = feed_rows(normed, weights)
    return (mixed + feed).astype(jnp.bfloat16)


def solution(mesh):
    return jax.shard_map(
        per_device,
        mesh=mesh,
        in_specs=(
            P(("pair", "role", "shard"), None, None),
            P(("pair", "role", "shard"), None, None),
            P(("pair", "role", "shard"), None, None),
            P(("pair", "role", "shard"), None),
            P(("pair", "role", "shard"), None),
            P(("pair", "role", "shard")),
            P(("pair", "role", "shard"), None),
            P(),
            P("role", "shard"),
            P("role", "shard"),
            P("shard", "role"),
        ),
        out_specs=P(("pair", "role", "shard"), None),
        check_vma=False,
    )
```

profile of v0, /device:TPU:152, one launch (start us, length us, event | category | flops | bytes accessed | tf_op | source)
XLA Modules:
  0.0 366.8 jit_solution(5721240351623603844)
XLA Ops:
  6.5 0.0 copy-start
  6.5 0.0 copy-start.2
  6.5 0.0 copy-start.6
  6.5 0.0 all-gather.3.cloned.1.call-start
  6.5 0.8 iota_compare_fusion
  7.4 0.7 reshape.74
  8.1 1.0 fusion.20
  9.1 1.8 fusion.19
  11.0 0.2 fusion.8
  11.2 0.7 reshape.66
  11.9 1.5 fusion.2
  13.5 0.0 copy-done.2
  13.5 0.2 multiply_reduce_fusion
  13.7 0.0 copy-done.6
  13.7 0.2 multiply_convert_fusion
  13.9 7.9 %all_to_all.32 = bf16[6,2,4096]{2,0,1:T(8,128)(2,1)S(1)} all-to-all(bf16[6,2,4096]{2,0,1:T(8,128)(2,1)S(1)} %bitcast.49), channel_id=1, replica_groups=mesh['pair'=8,'role'=2,'shard'=32] {'role'}, dimensions={1} | all-to-all | bytes 196608 | tf_op jit(solution)/shard_map/all_to_all | solution.py:50
  21.8 0.7 reshape.68
  22.5 0.0 all-gather.3.cloned.1.call-update
  22.5 0.0 copy-start.3
  22.5 0.0 all-reduce.4.cloned.1.call-start
  22.6 103.5 %all-gather.3.cloned.1.call-done = bf16[32,12,4096]{2,1,0:T(8,128)(2,1)} async-done(((bf16[1,12,4096]{2,1,0:T(8,128)(2,1)}), bf16[32,12,4096]{2,1,0:T(8,128)(2,1)}) %all-gather.3.cloned.1.call-update) | async-done | bytes 3145744 | tf_op jit(solution)/shard_map/all_gather | solution.py:51
  126.1 5.6 %reshape.69 = bf16[384,4096]{1,0:T(8,128)(2,1)} reshape(bf16[32,12,4096]{2,1,0:T(8,128)(2,1)} %all-gather.3.cloned.1.call-done) | data formatting | bytes 6291456
  131.7 0.0 copy-done.3
  131.7 0.0 copy-start.1
  131.7 0.0 copy-start.4
  131.7 3.0 convolution_convert_fusion.1
  134.7 0.0 copy-done.1
  134.7 0.1 copy-done.4
  134.8 1.0 convolution_convert_fusion.2
  135.8 0.7 pad_maximum_fusion
  136.5 0.0 all-reduce.4.cloned.1.call-update
  136.5 36.7 %all-reduce.4.cloned.1.call-done = bf16[384,256]{0,1:T(8,128)(2,1)} async-done(((bf16[384,256]{0,1:T(8,128)(2,1)}), bf16[384,256]{0,1:T(8,128)(2,1)}) %all-reduce.4.cloned.1.call-update) | async-done | bytes 196624 | tf_op jit(solution)/shard_map/psum | solution.py:55
  173.2 1.0 convert_element_type.57
  174.2 0.0 copy-done
  174.2 2.7 convolution_convert_fusion
  176.8 99.7 %fusion = bf16[16,4096]{1,0:T(8,128)(2,1)S(1)} fusion(bf16[384,4096]{1,0:T(8,128)(2,1)} %convolution_convert_fusion), kind=kCustom, calls=%all-reduce-scatter | all-reduce-scatter fusion | flops 2097153 | bytes 3278848
  276.5 5.5 %collective-permute-start = (bf16[16,4096]{1,0:T(8,128)(2,1)S(1)}, bf16[16,4096]{1,0:T(8,128)(2,1)S(1)}, u32[]{:S(2)}, u32[]{:S(2)}) collective-permute-start(bf16[16,4096]{1,0:T(8,128)(2,1)S(1)} %fusion), channel_id=1, source_target_pairs={{0,1},{1,2},{2,3},{3,4},{4,5},{5,6},{6,7},{7,8},{8,9},{9,10},{10,1... | collective-permute-start | bytes 393224
  282.0 9.3 %collective-permute-start.1 = (bf16[16,4096]{1,0:T(8,128)(2,1)S(1)}, bf16[16,4096]{1,0:T(8,128)(2,1)S(1)}, u32[]{:S(2)}, u32[]{:S(2)}) collective-permute-start(bf16[16,4096]{1,0:T(8,128)(2,1)S(1)} %fusion), channel_id=1, source_target_pairs={{0,2},{1,3},{2,4},{3,5},{4,6},{5,7},{6,8},{7,9},{8,10},{9,11},{10,... | collective-permute-start | bytes 393224
  291.3 1.9 collective-permute-start.7
  293.2 13.9 %collective-permute-start.2 = (bf16[16,4096]{1,0:T(8,128)(2,1)S(1)}, bf16[16,4096]{1,0:T(8,128)(2,1)S(1)}, u32[]{:S(2)}, u32[]{:S(2)}) collective-permute-start(bf16[16,4096]{1,0:T(8,128)(2,1)S(1)} %fusion), channel_id=1, source_target_pairs={{0,3},{1,4},{2,5},{3,6},{4,7},{5,8},{6,9},{7,10},{8,11},{9,12},{10... | collective-permute-start | bytes 393224
  307.1 1.9 collective-permute-start.3
  309.0 0.0 collective-permute-done.7
  309.1 22.4 %collective-permute-start.4 = (bf16[16,4096]{1,0:T(8,128)(2,1)S(1)}, bf16[16,4096]{1,0:T(8,128)(2,1)S(1)}, u32[]{:S(2)}, u32[]{:S(2)}) collective-permute-start(bf16[16,4096]{1,0:T(8,128)(2,1)S(1)} %fusion), channel_id=1, source_target_pairs={{0,5},{1,6},{2,7},{3,8},{4,9},{5,10},{6,11},{7,12},{8,13},{9,14},{... | collective-permute-start | bytes 393224
  331.4 0.0 collective-permute-done
  331.4 1.9 collective-permute-start.5
  333.4 0.0 collective-permute-done.1
  333.4 1.9 collective-permute-start.6
  335.3 1.3 dynamic-slice.4
  337.2 0.0 collective-permute-done.2
  337.2 0.0 collective-permute-done.3
  337.3 0.0 collective-permute-done.4
  337.3 5.4 %collective-permute-done.5 = bf16[16,4096]{1,0:T(8,128)(2,1)S(1)} collective-permute-done((bf16[16,4096]{1,0:T(8,128)(2,1)S(1)}, bf16[16,4096]{1,0:T(8,128)(2,1)S(1)}, u32[]{:S(2)}, u32[]{:S(2)}) %collective-permute-start.5) | collective-permute-done | bytes 131104
  342.7 0.0 copy-start.5
  342.7 0.7 copy-done.5
  343.3 2.6 collective-permute-done.6
  345.9 5.5 %concatenate.5 = bf16[140,4096]{1,0:T(8,128)(2,1)S(1)} concatenate(bf16[12,4096]{1,0:T(8,128)(2,1)S(1)} %collective-permute-done.7, bf16[16,4096]{1,0:T(8,128)(2,1)} %collective-permute-done.6, bf16[16,4096]{1,0:T(8,128)(2,1)} %copy-done.5, bf16[16,4096]{1,0:T(8,128)(2,1)S(1)} %collective-permute-done.4, bf16[16,4096]{1,0:T(8,128)(2,1)S(1)} %collective-permute-done.3, ...), dimensions={0} | concatenate | bytes 2293760
  351.6 7.6 %all_to_all.33 = bf16[2,6,4096]{2,1,0:T(8,128)(2,1)S(1)} all-to-all(bf16[2,6,4096]{2,1,0:T(8,128)(2,1)S(1)} %all_to_all.28), channel_id=1, replica_groups=mesh['pair'=8,'role'=2,'shard'=32] {'role'}, dimensions={0} | all-to-all | bytes 196608 | tf_op jit(solution)/shard_map/all_to_all | solution.py:63
  359.2 0.8 add_convert_fusion
  (7 shorter events, 0.2 us)
Async XLA Ops:
  6.5 167.6 %copy-start = (bf16[128,4096]{1,0:T(8,128)(2,1)S(1)}, bf16[128,4096]{1,0:T(8,128)(2,1)}, u32[]{:S(2)}) copy-start(bf16[128,4096]{1,0:T(8,128)(2,1)} %param.21) | copy-start | bytes 3145732
  6.5 6.9 %copy-start.2 = (bf16[6,8192]{1,0:T(8,128)(2,1)S(1)}, bf16[6,8192]{1,0:T(8,128)(2,1)}, u32[]{:S(2)}) copy-start(bf16[6,8192]{1,0:T(8,128)(2,1)} %param.17) | copy-start | bytes 294916
  6.5 7.2 %copy-start.6 = (f32[8192]{0:T(1024)S(1)}, f32[8192]{0:T(1024)}, u32[]{:S(2)}) copy-start(f32[8192]{0:T(1024)} %param.18) | copy-start | bytes 98308
  6.5 119.5 %all-gather.3.cloned.1.call-start = ((), (), s32[]{:S(2)}) async-start(), calls=%async_computation.3 | async-start | bytes 4325376 | tf_op jit(solution)/shard_map/all_gather | solution.py:51
  22.5 109.2 %copy-start.3 = (bf16[4096,128]{1,0:T(8,128)(2,1)S(1)}, bf16[4096,128]{1,0:T(8,128)(2,1)}, u32[]{:S(2)}) copy-start(bf16[4096,128]{1,0:T(8,128)(2,1)} %param.20) | copy-start | bytes 3145732
  22.5 150.7 %all-reduce.4.cloned.1.call-start = ((), (), s32[]{:S(2)}) async-start(), calls=%async_computation.2 | async-start | bytes 393216 | tf_op jit(solution)/shard_map/psum | solution.py:55
  131.7 3.0 copy-start.1
  131.7 3.1 copy-start.4
  276.5 54.9 %collective-permute-start = (bf16[16,4096]{1,0:T(8,128)(2,1)S(1)}, bf16[16,4096]{1,0:T(8,128)(2,1)S(1)}, u32[]{:S(2)}, u32[]{:S(2)}) collective-permute-start(bf16[16,4096]{1,0:T(8,128)(2,1)S(1)} %fusion), channel_id=1, source_target_pairs={{0,1},{1,2},{2,3},{3,4},{4,5},{5,6},{6,7},{7,8},{8,9},{9,10},{10,1... | collective-permute-start | bytes 393224
  282.0 51.4 %collective-permute-start.1 = (bf16[16,4096]{1,0:T(8,128)(2,1)S(1)}, bf16[16,4096]{1,0:T(8,128)(2,1)S(1)}, u32[]{:S(2)}, u32[]{:S(2)}) collective-permute-start(bf16[16,4096]{1,0:T(8,128)(2,1)S(1)} %fusion), channel_id=1, source_target_pairs={{0,2},{1,3},{2,4},{3,5},{4,6},{5,7},{6,8},{7,9},{8,10},{9,11},{10,... | collective-permute-start | bytes 393224
  291.3 17.8 %collective-permute-start.7 = (bf16[12,4096]{1,0:T(8,128)(2,1)S(1)}, bf16[12,4096]{1,0:T(8,128)(2,1)S(1)}, u32[]{:S(2)}, u32[]{:S(2)}) collective-permute-start(bf16[12,4096]{1,0:T(8,128)(2,1)S(1)} %slice.10), channel_id=1, source_target_pairs={{0,8},{1,9},{2,10},{3,11},{4,12},{5,13},{6,14},{7,15},{8,16},{9,17... | collective-permute-start | bytes 294920
  293.2 44.0 %collective-permute-start.2 = (bf16[16,4096]{1,0:T(8,128)(2,1)S(1)}, bf16[16,4096]{1,0:T(8,128)(2,1)S(1)}, u32[]{:S(2)}, u32[]{:S(2)}) collective-permute-start(bf16[16,4096]{1,0:T(8,128)(2,1)S(1)} %fusion), channel_id=1, source_target_pairs={{0,3},{1,4},{2,5},{3,6},{4,7},{5,8},{6,9},{7,10},{8,11},{9,12},{10... | collective-permute-start | bytes 393224
  307.1 30.1 %collective-permute-start.3 = (bf16[16,4096]{1,0:T(8,128)(2,1)S(1)}, bf16[16,4096]{1,0:T(8,128)(2,1)S(1)}, u32[]{:S(2)}, u32[]{:S(2)}) collective-permute-start(bf16[16,4096]{1,0:T(8,128)(2,1)S(1)} %fusion), channel_id=1, source_target_pairs={{0,4},{1,5},{2,6},{3,7},{4,8},{5,9},{6,10},{7,11},{8,12},{9,13},{1... | collective-permute-start | bytes 393224
  309.1 28.2 %collective-permute-start.4 = (bf16[16,4096]{1,0:T(8,128)(2,1)S(1)}, bf16[16,4096]{1,0:T(8,128)(2,1)S(1)}, u32[]{:S(2)}, u32[]{:S(2)}) collective-permute-start(bf16[16,4096]{1,0:T(8,128)(2,1)S(1)} %fusion), channel_id=1, source_target_pairs={{0,5},{1,6},{2,7},{3,8},{4,9},{5,10},{6,11},{7,12},{8,13},{9,14},{... | collective-permute-start | bytes 393224
  331.4 11.2 %collective-permute-start.5 = (bf16[16,4096]{1,0:T(8,128)(2,1)S(1)}, bf16[16,4096]{1,0:T(8,128)(2,1)S(1)}, u32[]{:S(2)}, u32[]{:S(2)}) collective-permute-start(bf16[16,4096]{1,0:T(8,128)(2,1)S(1)} %fusion), channel_id=1, source_target_pairs={{0,6},{1,7},{2,8},{3,9},{4,10},{5,11},{6,12},{7,13},{8,14},{9,15},... | collective-permute-start | bytes 393224
  333.4 12.6 %collective-permute-start.6 = (bf16[16,4096]{1,0:T(8,128)(2,1)S(1)}, bf16[16,4096]{1,0:T(8,128)(2,1)}, u32[]{:S(2)}, u32[]{:S(2)}) collective-permute-start(bf16[16,4096]{1,0:T(8,128)(2,1)S(1)} %fusion), channel_id=1, source_target_pairs={{0,7},{1,8},{2,9},{3,10},{4,11},{5,12},{6,13},{7,14},{8,15},{9,16}... | collective-permute-start | bytes 393224
  342.7 0.7 copy-start.5
Sparse Core Ops, SparseCore 0:
  22.6 103.3 all-gather.2
  136.6 36.5 all-reduce.3
where the time goes:
time: 368 us; the launch traced here: 367 us
  waiting for transfers between devices  148 us (40%)
  blocking collectives  115 us (31%)
  starting transfers between devices  58.7 us (16%)
  local copies, waits for them, and re-layouts  15.4 us (4%)
  between operations  14.3 us (4%)
  matrix products  11.1 us (3%)
  other arithmetic  3.97 us (1%)
    all_gather x1, waiting for transfers between devices, feed_rows(): piece = lax.all_gather(halves, 'shard', axis=0, tiled=True)  103 us
    unnamed x1, blocking collectives  99.7 us
    unnamed x8, starting transfers between devices  58.7 us
    psum x1, waiting for transfers between devices, feed_rows(): both = lax.psum(both.astype(jnp.bfloat16), 'role').astype(jnp.float32)  36.7 us
    unnamed x20, local copies, waits for them, and re-layouts  13.9 us
    unnamed x10, waiting for transfers between devices  8.06 us
    all_to_all x1, blocking collectives, feed_rows(): lax.all_to_all(normed, 'role', split_axis=1, concat_axis=0, tiled=True)  7.91 us
    all_to_all x1, blocking collectives, feed_rows(): lax.all_to_all(mine.astype(jnp.bfloat16), 'role', split_axis=0, concat_ax...  7.6 us
  transfers between devices with their start and end apart: 10, of which 4 were waited for; matrix products, arithmetic and copies ran while one was open for 0% of the time, Pallas kernels for 0%

commit v1 on v0

v1 whole, which is shorter than its diff:
```python
import jax
import jax.numpy as jnp
from jax import lax
from jax.experimental import pallas as pl
from jax.experimental.pallas import tpu as pltpu
from jax.sharding import PartitionSpec as P

MESH = pl.DeviceIdType.MESH
F32 = jnp.float32
BF16 = jnp.bfloat16
R = 6
HD = 128
QH = 64
KVH = 4
GRP = QH // KVH
L = 128
N = 8
ROWS = R * N
FB = 1024
HB = 128
NB = 4
HALF = FB // 2


def mod(a, n):
    return lax.rem(a + 4 * n, n)


def kernel(
    q_ref, nk_ref, nv_ref, len_ref, res_ref, gain_ref, ck_hbm, cv_hbm, gate_hbm, up_hbm, down_hbm,
    out_ref,
    ck, cv, wgu, wd, scores, mixed, natural, n_send, n_recv, relay, acts, rz_send, rz_recv, hid, ry_send, ry_recv,
    f_send, f_recv,
    cache_sem, own_sem, wz_ssem, wz_rsem, wx_ssem, wx_rsem, wc_ssem, wc_rsem, a1_ssem, a1_rsem, ag_ssem, ag_rsem,
    rz_ssem, rz_rsem, hg_ssem, hg_rsem, ry_ssem, ry_rsem, a2_ssem, a2_rsem,
):
    pair, role, shard = lax.axis_index("pair"), lax.axis_index("role"), lax.axis_index("shard")
    x, c = pair // 2, lax.rem(pair, 2)
    z_hi, y = shard // 8, lax.rem(shard, 8)
    z = z_hi * 2 + role

    def at_z(k):
        to = mod(z + k, 8)
        return (pair, lax.rem(to, 2), (to // 2) * 8 + y)

    def at_y(k):
        return (pair, role, z_hi * 8 + mod(y + k, 8))

    def at_x(k):
        return (mod(x + k, 4) * 2 + c, role, shard)

    sibling = (x * 2 + (1 - c), role, shard)

    sends = []

    def push(src, dst, ssem, rsem, to):
        copy = pltpu.make_async_remote_copy(
            src_ref=src, dst_ref=dst, send_sem=ssem, recv_sem=rsem, device_id=to, device_id_type=MESH
        )
        copy.start()
        sends.append(copy)
        return copy

    locals_ = []
    for i, (src, dst) in enumerate(((ck_hbm, ck), (cv_hbm, cv))):
        copy = pltpu.make_async_copy(src, dst, cache_sem.at[i])
        copy.start()
        locals_.append(copy)
    quarter = pl.ds(pl.multiple_of(z_hi * FB, FB), FB)
    own = []
    for i, (src, dst) in enumerate((
        (gate_hbm.at[quarter, :], wgu.at[0, :, pl.ds(0, HB)]),
        (up_hbm.at[quarter, :], wgu.at[0, :, pl.ds(HB, HB)]),
        (down_hbm.at[:, quarter], wd.at[0]),
    )):
        copy = pltpu.make_async_copy(src, dst, own_sem.at[i])
        copy.start()
        own.append(copy)

    barrier = pltpu.get_barrier_semaphore()
    partners = [at_z(k) for k in range(1, 8)] + [at_y(1), at_y(-1)] + [at_x(k) for k in range(1, 4)] + [sibling]
    for to in partners:
        pl.semaphore_signal(barrier, inc=1, device_id=to, device_id_type=MESH)
    pl.semaphore_wait(barrier, len(partners))

    p = c * 4 + x
    p_gu = pl.ds(pl.multiple_of(p * 128, 128), 128)
    p_d = pl.ds(pl.multiple_of(p * 16, 16), 16)
    wz = []
    for k in (1, 3, 2):
        q_to = mod(z_hi + k, 4)
        rows = pl.ds(pl.multiple_of(q_to * FB + p * 128, 128), 128)
        cols = pl.ds(pl.multiple_of(q_to * FB, FB), FB)
        to = (pair, role, q_to * 8 + y)
        for i, (src, dst) in enumerate((
            (gate_hbm.at[rows, :], wgu.at[4 - k, p_gu, pl.ds(0, HB)]),
            (up_hbm.at[rows, :], wgu.at[4 - k, p_gu, pl.ds(HB, HB)]),
            (down_hbm.at[p_d, cols], wd.at[4 - k, p_d, :]),
        )):
            wz.append((i, push(src, dst, wz_ssem.at[k - 1, i], wz_rsem.at[k - 1, i], to)))

    locals_[0].wait()
    for r in range(R):
        for k in range(KVH):
            scores[pl.ds(QH * r + GRP * k, GRP), :] = lax.dot_general(
                q_ref[r, pl.ds(GRP * k, GRP), :], ck[r, :, pl.ds(HD * k, HD)],
                (((1,), (1,)), ((), ())), preferred_element_type=F32,
            )

    for i, copy in wz:
        if i < 2:
            copy.wait_recv()
    part_gu = wgu.at[pl.ds(1, 3), p_gu, :]
    part_d = wd.at[pl.ds(1, 3), p_d, :]
    wx_gu = [push(part_gu, part_gu, wx_ssem.at[k - 1, 0], wx_rsem.at[k - 1, 0], at_x(k)) for k in (1, 3, 2)]

    for i in range(QH):
        mixed[pl.ds(i, R, stride=QH), :] = res_ref[:, pl.ds(HD * i, HD)].astype(F32)
    locals_[1].wait()
    scale = F32(1.0) / jnp.sqrt(F32(HD))
    slot = lax.broadcasted_iota(jnp.int32, (QH, L), 1)
    for r in range(R):
        rows = pl.ds(QH * r, QH)
        keys = [jnp.broadcast_to(nk_ref[pl.ds(r, 1), pl.ds(HD * k, HD)].astype(F32), (GRP, HD)) for k in range(KVH)]
        vals = [jnp.broadcast_to(nv_ref[pl.ds(r, 1), pl.ds(HD * k, HD)].astype(F32), (GRP, HD)) for k in range(KVH)]
        own_score = jnp.sum(q_ref[r].astype(F32) * jnp.concatenate(keys, 0), axis=1, keepdims=True) * scale
        valid = slot < len_ref[r]
        kept = jnp.where(valid, scores[rows, :] * scale, F32(-1e30))
        top = jnp.maximum(jnp.max(kept, axis=1, keepdims=True), own_score)
        weights = jnp.where(valid, jnp.exp(kept - top), F32(0.0))
        own_weight = jnp.exp(own_score - top)
        total = jnp.sum(weights, axis=1, keepdims=True) + own_weight
        low = weights.astype(BF16)
        summed = jnp.concatenate(
            [
                jnp.dot(low[GRP * k:GRP * (k + 1)], cv[r, :, pl.ds(HD * k, HD)], preferred_element_type=F32)
                for k in range(KVH)
            ], 0,
        )
        summed = summed + own_weight.astype(BF16).astype(F32) * jnp.concatenate(vals, 0)
        mix = mixed[rows, :] + summed / total
        mixed[rows, :] = mix
        mean = jnp.sum(jnp.sum(mix * mix, axis=1, keepdims=True), axis=0, keepdims=True) * F32(1.0 / (QH * HD))
        natural[rows, :] = mix * lax.rsqrt(mean + F32(1e-5)) * gain_ref[...]

    for e in range(N):
        n_send[e] = jnp.concatenate([natural[pl.ds(QH * r + 8 * e, 8), :] for r in range(R)], 0).astype(BF16)

    def tile_of(at):
        return lax.rem(at, 2) * 4 + at // 2

    a1 = [
        push(n_send.at[tile_of(mod(z + k, 8))], n_recv.at[z], a1_ssem.at[k - 1], a1_rsem.at[k - 1], at_z(k))
        for k in (4, 3, 5, 2, 6, 1, 7)
    ]
    n_recv[z] = n_send[tile_of(z)]
    for copy in a1:
        copy.wait_recv()
    relay[...] = n_recv[...].reshape(N * ROWS, HD).astype(F32)
    acts[y] = jnp.concatenate([relay[pl.ds(i, ROWS, stride=8), :] for i in range(8)], 1).astype(BF16)

    def gather(buf, me, at, ssem, rsem, width, between):
        half = width // 2
        arrivals = {}
        for t in range(4):
            for s in range(2):
                for way, sign in ((0, 1), (1, -1)):
                    if t:
                        arrivals[way, t - 1, s].wait_recv()
                    if t == 3 and s != way:
                        continue
                    ref = buf.at[mod(me - sign * t, 8), :, pl.ds(s * half, half)]
                    arrivals[way, t, s] = push(ref, ref, ssem.at[way, t, s], rsem.at[way, t, s], at(sign))
            between(t)
        for way in range(2):
            arrivals[way, 3, way].wait_recv()

    def scatter(term, me, at, ssem, rsem, sbuf, rbuf, between):
        arrivals = {}
        for t in range(4):
            for way, sign in ((0, 1), (1, -1)):
                target = mod(me + sign * (4 - t), 8)
                for s in range(2):
                    cols = pl.ds(s * HALF, HALF)
                    if t == 0 and s != way:
                        continue
                    value = term(target, s)
                    if (way, t - 1, s) in arrivals:
                        arrivals[way, t - 1, s].wait_recv()
                        value = value + rbuf[way, t - 1, :, cols].astype(F32)
                    sbuf[way, t, :, cols] = value.astype(BF16)
                    arrivals[way, t, s] = push(
                        sbuf.at[way, t, :, cols], rbuf.at[way, t, :, cols],
                        ssem.at[way, t, s], rsem.at[way, t, s], at(sign),
                    )
            between(t)
        out = []
        for s in range(2):
            cols = pl.ds(s * HALF, HALF)
            value = term(me, s)
            for way in range(2):
                arrivals[way, 3, s].wait_recv()
                value = value + rbuf[way, 3, :, cols].astype(F32)
            out.append(value)
        return out

    wx_d, wc = [], []

    def pass_weights(t):
        if t == 0:
            for i, copy in wz:
                if i == 2:
                    copy.wait_recv()
            wx_d.extend(push(part_d, part_d, wx_ssem.at[k - 1, 1], wx_rsem.at[k - 1, 1], at_x(k)) for k in (1, 3, 2))
        if t == 2:
            for copy in wx_gu:
                copy.wait_recv()
            ref = wgu.at[pl.ds(1, 3), pl.ds(pl.multiple_of(c * 512, 512), 512), :]
            wc.append(push(ref, ref, wc_ssem.at[0], wc_rsem.at[0], sibling))

    gather(acts, y, at_y, ag_ssem, ag_rsem, FB, pass_weights)
    own[0].wait()
    own[1].wait()
    wc[0].wait_recv()

    def gate_up(target, s):
        rows = acts[target]
        return jnp.concatenate(
            [
                jnp.dot(rows, wgu[mod(b - z_hi, 4)], preferred_element_type=F32)
                for b in (2 * s, 2 * s + 1)
            ], 1,
        )

    def pass_down(t):
        if t == 0:
            for copy in wx_d:
                copy.wait_recv()
            ref = wd.at[pl.ds(1, 3), pl.ds(pl.multiple_of(c * 64, 64), 64), :]
            wc.append(push(ref, ref, wc_ssem.at[1], wc_rsem.at[1], sibling))

    both = scatter(gate_up, z, at_z, rz_ssem, rz_rsem, rz_send, rz_recv, pass_down)
    hidden = []
    for s in range(2):
        for b in range(2):
            gate = both[s][:, 256 * b:256 * b + HB]
            up = both[s][:, 256 * b + HB:256 * (b + 1)]
            hidden.append((gate / (F32(1.0) + jnp.exp(-gate)) * up).astype(BF16))
    hid[z] = jnp.concatenate(hidden, 1)

    gather(hid, z, at_z, hg_ssem, hg_rsem, NB * HB, lambda t: None)
    own[2].wait()
    wc[1].wait_recv()

    def down_term(target, s):
        rows = hid[target]
        total = None
        for b in range(NB):
            term = jnp.dot(
                rows[:, HB * b:HB * (b + 1)], wd[mod(b - z_hi, 4), :, pl.ds(s * HALF, HALF)], preferred_element_type=F32
            )
            total = term if total is None else total + term
        return total

    feed = scatter(down_term, y, at_y, ry_ssem, ry_rsem, ry_send, ry_recv, lambda t: None)
    feed = jnp.concatenate(feed, 1)
    for i in range(8):
        relay[pl.ds(i, ROWS, stride=8), :] = feed[:, HD * i:HD * (i + 1)]
    f_send[...] = relay[...].astype(BF16).reshape(N, ROWS, HD)
    me = tile_of(z)
    a2 = [
        push(f_send.at[mod(z + k, 8)], f_recv.at[me], a2_ssem.at[k - 1], a2_rsem.at[k - 1], at_z(k))
        for k in (4, 3, 5, 2, 6, 1, 7)
    ]
    f_recv[me] = f_send[z]
    for copy in a2:
        copy.wait_recv()
    for e in range(N):
        mix = jnp.concatenate([mixed[pl.ds(QH * r + 8 * e, 8), :] for r in range(R)], 0)
        natural[pl.ds(ROWS * e, ROWS), :] = mix + f_recv[e].astype(F32)
    for e in range(N):
        for i in range(8):
            out_ref[:, pl.ds(FB * e + HD * i, HD)] = natural[pl.ds(ROWS * e + i, R, stride=8), :].astype(BF16)
    for copy in sends:
        copy.wait_send()


def per_device(q, ck, cv, nk, nv, lengths, residual, gain, gate, up, down):
    vmem = pl.BlockSpec(memory_space=pltpu.VMEM)
    smem = pl.BlockSpec(memory_space=pltpu.SMEM)
    hbm = pl.BlockSpec(memory_space=pl.ANY)
    dma = pltpu.SemaphoreType.DMA
    ring = (2, 4, 2)
    return pl.pallas_call(
        kernel,
        out_shape=jax.ShapeDtypeStruct((R, QH * HD), BF16),
        in_specs=[vmem, vmem, vmem, smem, vmem, vmem, hbm, hbm, hbm, hbm, hbm],
        out_specs=vmem,
        scratch_shapes=[
            pltpu.VMEM((R, L, KVH * HD), BF16),
            pltpu.VMEM((R, L, KVH * HD), BF16),
            pltpu.VMEM((NB, FB, 2 * HB), BF16),
            pltpu.VMEM((NB, HB, FB), BF16),
            pltpu.VMEM((R * QH, L), F32),
            pltpu.VMEM((R * QH, HD), F32),
            pltpu.VMEM((R * QH, HD), F32),
            pltpu.VMEM((N, ROWS, HD), BF16),
            pltpu.VMEM((N, ROWS, HD), BF16),
            pltpu.VMEM((N * ROWS, HD), F32),
            pltpu.VMEM((N, ROWS, FB), BF16),
            pltpu.VMEM((2, 4, ROWS, FB), BF16),
            pltpu.VMEM((2, 4, ROWS, FB), BF16),
            pltpu.VMEM((N, ROWS, NB * HB), BF16),
            pltpu.VMEM((2, 4, ROWS, FB), BF16),
            pltpu.VMEM((2, 4, ROWS, FB), BF16),
            pltpu.VMEM((N, ROWS, HD), BF16),
            pltpu.VMEM((N, ROWS, HD), BF16),
            dma((2,)), dma((3,)),
            dma((3, 3)), dma((3, 3)),
            dma((3, 2)), dma((3, 2)),
            dma((2,)), dma((2,)),
            dma((7,)), dma((7,)),
            dma(ring), dma(ring),
            dma(ring), dma(ring),
            dma(ring), dma(ring),
            dma(ring), dma(ring),
            dma((7,)), dma((7,)),
        ],
        compiler_params=pltpu.CompilerParams(
            collective_id=0, has_side_effects=True, vmem_limit_bytes=48 * 1024 * 1024
        ),
        cost_estimate=pl.CostEstimate(flops=1_400_000_000, bytes_accessed=5_000_000, transcendentals=100_000),
    )(q, nk, nv, lengths, residual, gain.reshape(QH, HD), ck, cv, gate, up, down)


def solution(mesh):
    rows = ("pair", "role", "shard")
    return jax.shard_map(
        per_device,
        mesh=mesh,
        in_specs=(
            P(rows, None, None), P(rows, None, None), P(rows, None, None), P(rows, None), P(rows, None), P(rows),
            P(rows, None), P(), P("role", "shard"), P("role", "shard"), P("shard", "role"),
        ),
        out_specs=P(rows, None),
        check_vma=False,
    )
```

time: 368 us -> 108 us (0.29)
  the two profiles are of different devices: /device:TPU:152 before, /device:TPU:8 now
where the time goes in v1:
time: 108 us
  Pallas kernels  96.4 us (89%)
  local copies, waits for them, and re-layouts  11.2 us (10%)
    pallas_call x1, Pallas kernels, per_device(): pl.pallas_call(kernel, out_shape=jax.ShapeDtypeStruct((R, QH * HD), BF16)...  96.4 us
    unnamed x23, local copies, waits for them, and re-layouts  11.2 us

profile of v1, /device:TPU:8, one launch (start us, length us, event | category | flops | bytes accessed | tf_op | source)
XLA Modules:
  0.0 107.6 jit_solution(8308423592837535311)
XLA Ops:
  0.0 0.0 copy-start.10
  0.0 0.7 copy-done.10
  0.7 0.0 copy-start
  0.7 1.2 %copy-done = bf16[4096,128]{1,0:T(8,128)(2,1)S(1)} copy-done((bf16[4096,128]{1,0:T(8,128)(2,1)S(1)}, bf16[4096,128]{1,0:T(8,128)(2,1)}, u32[]{:S(2)}) %copy-start) | copy-done | bytes 1048600
  1.9 0.0 copy-start.1
  1.9 1.2 %copy-done.1 = bf16[4096,128]{1,0:T(8,128)(2,1)S(1)} copy-done((bf16[4096,128]{1,0:T(8,128)(2,1)S(1)}, bf16[4096,128]{1,0:T(8,128)(2,1)}, u32[]{:S(2)}) %copy-start.1) | copy-done | bytes 1048600
  3.1 0.0 copy-start.2
  3.1 1.2 %copy-done.2 = bf16[128,4096]{1,0:T(8,128)(2,1)S(1)} copy-done((bf16[128,4096]{1,0:T(8,128)(2,1)S(1)}, bf16[128,4096]{1,0:T(8,128)(2,1)}, u32[]{:S(2)}) %copy-start.2) | copy-done | bytes 1048600
  4.3 0.0 copy-start.3
  4.3 1.1 %copy-done.3 = bf16[6,128,512]{2,1,0:T(8,128)(2,1)S(1)} copy-done((bf16[6,128,512]{2,1,0:T(8,128)(2,1)S(1)}, bf16[6,128,512]{2,1,0:T(8,128)(2,1)}, u32[]{:S(2)}) %copy-start.3) | copy-done | bytes 786456
  5.5 0.0 copy-start.4
  5.5 1.1 %copy-done.4 = bf16[6,128,512]{2,1,0:T(8,128)(2,1)S(1)} copy-done((bf16[6,128,512]{2,1,0:T(8,128)(2,1)S(1)}, bf16[6,128,512]{2,1,0:T(8,128)(2,1)}, u32[]{:S(2)}) %copy-start.4) | copy-done | bytes 786456
  6.6 0.0 copy-start.5
  6.6 0.9 copy-done.5
  7.5 0.0 copy-start.6
  7.5 0.9 copy-done.6
  8.4 0.0 copy-start.7
  8.4 0.8 copy-done.7
  9.2 0.0 copy-start.8
  9.2 0.7 copy-done.8
  9.9 0.0 copy-start.9
  9.9 0.7 copy-done.9
  10.6 96.4 %shard_map.109 = bf16[6,8192]{1,0:T(8,128)(2,1)S(1)} custom-call(bf16[6,64,128]{2,1,0:T(8,128)(2,1)S(1)} %copy-done.6, bf16[6,512]{1,0:T(8,128)(2,1)S(1)} %copy-done.8, bf16[6,512]{1,0:T(8,128)(2,1)S(1)} %copy-done.9, s32[6]{0:T(128)S(1)} %copy-done.10, bf16[6,8192]{1,0:T(8,128)(2,1)S(1)} %copy-done.5, f32[64,128]{1,0:T(8,128)S(1)} %bitcast.1, ...), custom_call_target="tpu_custom_call" | custom-call | flops 1400000000 | bytes 5000000 | tf_op jit(solution)/shard_map/pallas_call | solution.py:294
  107.0 0.7 copy.13
Async XLA Ops:
  0.0 0.7 copy-start.10
  0.7 1.2 %copy-start = (bf16[4096,128]{1,0:T(8,128)(2,1)S(1)}, bf16[4096,128]{1,0:T(8,128)(2,1)}, u32[]{:S(2)}) copy-start(bf16[4096,128]{1,0:T(8,128)(2,1)} %gate_hbm.1) | copy-start | bytes 3145732
  1.9 1.2 %copy-start.1 = (bf16[4096,128]{1,0:T(8,128)(2,1)S(1)}, bf16[4096,128]{1,0:T(8,128)(2,1)}, u32[]{:S(2)}) copy-start(bf16[4096,128]{1,0:T(8,128)(2,1)} %up_hbm.1) | copy-start | bytes 3145732
  3.1 1.2 %copy-start.2 = (bf16[128,4096]{1,0:T(8,128)(2,1)S(1)}, bf16[128,4096]{1,0:T(8,128)(2,1)}, u32[]{:S(2)}) copy-start(bf16[128,4096]{1,0:T(8,128)(2,1)} %down_hbm.1) | copy-start | bytes 3145732
  4.3 1.1 %copy-start.3 = (bf16[6,128,512]{2,1,0:T(8,128)(2,1)S(1)}, bf16[6,128,512]{2,1,0:T(8,128)(2,1)}, u32[]{:S(2)}) copy-start(bf16[6,128,512]{2,1,0:T(8,128)(2,1)} %ck_hbm.1) | copy-start | bytes 2359300
  5.5 1.1 %copy-start.4 = (bf16[6,128,512]{2,1,0:T(8,128)(2,1)S(1)}, bf16[6,128,512]{2,1,0:T(8,128)(2,1)}, u32[]{:S(2)}) copy-start(bf16[6,128,512]{2,1,0:T(8,128)(2,1)} %cv_hbm.1) | copy-start | bytes 2359300
  6.6 0.9 copy-start.5
  7.5 0.9 copy-start.6
  8.4 0.8 copy-start.7
  9.2 0.7 copy-start.8
  9.9 0.7 copy-start.9

commit v2 on v1

v2 whole, which is shorter than its diff:
```python
import jax
import jax.numpy as jnp
from jax import lax
from jax.experimental import pallas as pl
from jax.experimental.pallas import tpu as pltpu
from jax.sharding import PartitionSpec as P

MESH = pl.DeviceIdType.MESH
F32 = jnp.float32
BF16 = jnp.bfloat16
R = 6
HD = 128
QH = 64
KVH = 4
GRP = QH // KVH
L = 128
N = 8
ROWS = R * N
FB = 1024
HB = 128
NB = 4
HALF = FB // 2


def mod(a, n):
    return lax.rem(a + 4 * n, n)


def kernel(
    len_ref, q_hbm, ck_hbm, cv_hbm, nk_hbm, nv_hbm, res_hbm, gain_hbm, gate_hbm, up_hbm, down_hbm,
    out_ref,
    q_ref, ck, cv, nk_ref, nv_ref, res_ref, gain_ref, wgu, wd, scores, mixed, natural, n_send, n_recv, relay,
    acts, rz_send, rz_recv, hid, ry_send, ry_recv, f_send, f_recv,
    local_sem, own_sem, wz_ssem, wz_rsem, wx_ssem, wx_rsem, wc_ssem, wc_rsem, ready_sem, a1_ssem, a1_rsem, ag_ssem, ag_rsem,
    rz_ssem, rz_rsem, hg_ssem, hg_rsem, ry_ssem, ry_rsem, a2_ssem, a2_rsem,
):
    pair, role, shard = lax.axis_index("pair"), lax.axis_index("role"), lax.axis_index("shard")
    x, c = pair // 2, lax.rem(pair, 2)
    z_hi, y = shard // 8, lax.rem(shard, 8)
    z = z_hi * 2 + role

    def at_z(k):
        to = mod(z + k, 8)
        return (pair, lax.rem(to, 2), (to // 2) * 8 + y)

    def at_y(k):
        return (pair, role, z_hi * 8 + mod(y + k, 8))

    def at_x(k):
        return (mod(x + k, 4) * 2 + c, role, shard)

    sibling = (x * 2 + (1 - c), role, shard)

    def remote(src, dst, ssem, rsem, to):
        return pltpu.make_async_remote_copy(
            src_ref=src, dst_ref=dst, send_sem=ssem, recv_sem=rsem, device_id=to, device_id_type=MESH
        )

    operands = []
    for i, (src, dst) in enumerate((
        (q_hbm, q_ref), (ck_hbm, ck), (cv_hbm, cv), (nk_hbm, nk_ref), (nv_hbm, nv_ref), (res_hbm, res_ref), (gain_hbm, gain_ref),
    )):
        copy = pltpu.make_async_copy(src, dst, local_sem.at[i])
        copy.start()
        operands.append(copy)
    quarter = pl.ds(pl.multiple_of(z_hi * FB, FB), FB)
    own = []
    for i, (src, dst) in enumerate((
        (gate_hbm.at[quarter, :], wgu.at[0, :, pl.ds(0, HB)]),
        (up_hbm.at[quarter, :], wgu.at[0, :, pl.ds(HB, HB)]),
        (down_hbm.at[:, quarter], wd.at[0]),
    )):
        copy = pltpu.make_async_copy(src, dst, own_sem.at[i])
        copy.start()
        own.append(copy)

    barrier = pltpu.get_barrier_semaphore()

    def greet(to):
        pl.semaphore_signal(barrier, inc=1, device_id=to, device_id_type=MESH)

    for k in range(1, 8):
        greet(at_z(k))
        greet(at_y(k))

    @pl.when(c == 0)
    def _():
        for k in range(1, 4):
            greet(at_x(k))
        greet(sibling)
        pl.semaphore_wait(barrier, 17)

    @pl.when(c == 1)
    def _():
        pl.semaphore_wait(barrier, 15)
        pl.semaphore_signal(ready_sem, inc=1, device_id=sibling, device_id_type=MESH)

    part = pl.ds(pl.multiple_of(x * 256, 256), 256)
    part_d = pl.ds(pl.multiple_of(x * 32, 32), 32)

    def weight_z(k, i):
        q_to = mod(z_hi + k, 4)
        rows = pl.ds(pl.multiple_of(q_to * FB + x * 256, 256), 256)
        cols = pl.ds(pl.multiple_of(q_to * FB, FB), FB)
        src, dst = (
            (gate_hbm.at[rows, :], wgu.at[4 - k, part, pl.ds(0, HB)]),
            (up_hbm.at[rows, :], wgu.at[4 - k, part, pl.ds(HB, HB)]),
            (down_hbm.at[part_d, cols], wd.at[4 - k, part_d, :]),
        )[i]
        return remote(src, dst, wz_ssem.at[k - 1, i], wz_rsem.at[k - 1, i], (pair, role, q_to * 8 + y))

    def weight_x(k, to, i):
        ref = (wgu.at[4 - k, part, :], wd.at[4 - k, part_d, :])[i]
        return remote(ref, ref, wx_ssem.at[k - 1, to - 1, i], wx_rsem.at[k - 1, to - 1, i], at_x(to))

    def weight_c(i):
        ref = (wgu, wd)[i].at[pl.ds(1, 3)]
        return remote(ref, ref, wc_ssem.at[i], wc_rsem.at[i], sibling)

    @pl.when(c == 0)
    def _():
        for k in (1, 3, 2):
            weight_z(k, 0).start()
            weight_z(k, 1).start()

    def pass_gate_up(k):
        @pl.when(c == 0)
        def _():
            weight_z(k, 0).wait_recv()
            weight_z(k, 1).wait_recv()
            for to in (2, 1, 3):
                weight_x(k, to, 0).start()

    for copy in operands[:2]:
        copy.wait()
    for r in range(R):
        for k in range(KVH):
            scores[pl.ds(QH * r + GRP * k, GRP), :] = lax.dot_general(
                q_ref[r, pl.ds(GRP * k, GRP), :], ck[r, :, pl.ds(HD * k, HD)],
                (((1,), (1,)), ((), ())), preferred_element_type=F32,
            )
    for copy in operands[2:]:
        copy.wait()
    for i in range(QH):
        mixed[pl.ds(i, R, stride=QH), :] = res_ref[:, pl.ds(HD * i, HD)].astype(F32)
    scale = F32(1.0) / jnp.sqrt(F32(HD))
    slot = lax.broadcasted_iota(jnp.int32, (QH, L), 1)
    for r in range(R):
        if r in (2, 3, 4):
            pass_gate_up((1, 3, 2)[r - 2])
        rows = pl.ds(QH * r, QH)
        keys = [jnp.broadcast_to(nk_ref[pl.ds(r, 1), pl.ds(HD * k, HD)].astype(F32), (GRP, HD)) for k in range(KVH)]
        vals = [jnp.broadcast_to(nv_ref[pl.ds(r, 1), pl.ds(HD * k, HD)].astype(F32), (GRP, HD)) for k in range(KVH)]
        own_score = jnp.sum(q_ref[r].astype(F32) * jnp.concatenate(keys, 0), axis=1, keepdims=True) * scale
        valid = slot < len_ref[r]
        kept = jnp.where(valid, scores[rows, :] * scale, F32(-1e30))
        top = jnp.maximum(jnp.max(kept, axis=1, keepdims=True), own_score)
        weights = jnp.where(valid, jnp.exp(kept - top), F32(0.0))
        own_weight = jnp.exp(own_score - top)
        total = jnp.sum(weights, axis=1, keepdims=True) + own_weight
        low = weights.astype(BF16)
        summed = jnp.concatenate(
            [
                jnp.dot(low[GRP * k:GRP * (k + 1)], cv[r, :, pl.ds(HD * k, HD)], preferred_element_type=F32)
                for k in range(KVH)
            ], 0,
        )
        summed = summed + own_weight.astype(BF16).astype(F32) * jnp.concatenate(vals, 0)
        mix = mixed[rows, :] + summed / total
        mixed[rows, :] = mix
        mean = jnp.sum(jnp.sum(mix * mix, axis=1, keepdims=True), axis=0, keepdims=True) * F32(1.0 / (QH * HD))
        natural[rows, :] = mix * lax.rsqrt(mean + F32(1e-5)) * gain_ref[...]

    for e in range(N):
        n_send[e] = jnp.concatenate([natural[pl.ds(QH * r + 8 * e, 8), :] for r in range(R)], 0).astype(BF16)

    def tile_of(at):
        return lax.rem(at, 2) * 4 + at // 2

    far_first = (4, 3, 5, 2, 6, 1, 7)
    near_first = (1, 7, 2, 6, 3, 5, 4)
    a1 = [
        remote(n_send.at[tile_of(mod(z + k, 8))], n_recv.at[z], a1_ssem.at[k - 1], a1_rsem.at[k - 1], at_z(k))
        for k in far_first
    ]
    for copy in a1:
        copy.start()
    n_recv[z] = n_send[tile_of(z)]

    @pl.when(c == 0)
    def _():
        for k in (1, 3, 2):
            weight_z(k, 2).start()

    for copy in a1:
        copy.wait_recv()
    relay[...] = n_recv[...].reshape(N * ROWS, HD).astype(F32)
    acts[0] = jnp.concatenate([relay[pl.ds(i, ROWS, stride=8), :] for i in range(8)], 1).astype(BF16)

    ag = {k: remote(acts.at[0], acts.at[k], ag_ssem.at[k - 1], ag_rsem.at[k - 1], at_y(k)) for k in far_first}
    for k in far_first:
        ag[k].start()

    @pl.when(c == 0)
    def _():
        for k in (1, 3, 2):
            weight_z(k, 2).wait_recv()
            for to in (2, 1, 3):
                weight_x(k, to, 1).start()
        for k in (1, 3, 2):
            for to in (2, 1, 3):
                weight_x(k, to, 0).wait_recv()

    @pl.when(c == 1)
    def _():
        weight_c(0).wait_recv()

    own[0].wait()
    own[1].wait()

    def rz(k):
        return remote(rz_send.at[k], rz_recv.at[k], rz_ssem.at[k], rz_rsem.at[k], at_z(k))

    for n, k in enumerate((0,) + near_first):
        if k:
            ag[k].wait_recv()
        to = mod(y - k - z, 8)
        rows = acts[k]
        for b in range(NB):
            rz_send[to, :, pl.ds(2 * HB * b, 2 * HB)] = jnp.dot(
                rows, wgu[mod(b - z_hi, 4)], preferred_element_type=F32
            ).astype(BF16)

        @pl.when(to != 0)
        def _(to=to):
            rz(to).start()

        if n == 4:
            @pl.when(c == 0)
            def _():
                pl.semaphore_wait(ready_sem, 1)
                weight_c(0).start()

    for k in near_first:
        rz(k).wait_recv()
    for b in range(NB):
        cols = pl.ds(2 * HB * b, 2 * HB)
        both = rz_send[0, :, cols].astype(F32)
        for k in range(1, 8):
            both = both + rz_recv[k, :, cols].astype(F32)
        gate, up = both[:, :HB], both[:, HB:]
        hid[0, :, pl.ds(HB * b, HB)] = (gate / (F32(1.0) + jnp.exp(-gate)) * up).astype(BF16)

    hg = {k: remote(hid.at[0], hid.at[k], hg_ssem.at[k - 1], hg_rsem.at[k - 1], at_z(k)) for k in far_first}
    for k in far_first:
        hg[k].start()

    @pl.when(c == 0)
    def _():
        for k in (1, 3, 2):
            for to in (2, 1, 3):
                weight_x(k, to, 1).wait_recv()

    own[2].wait()

    @pl.when(c == 0)
    def _():
        weight_c(1).start()

    @pl.when(c == 1)
    def _():
        weight_c(1).wait_recv()

    def ry(k):
        return remote(ry_send.at[k], ry_recv.at[k], ry_ssem.at[k], ry_rsem.at[k], at_y(k))

    for k in (0,) + near_first:
        if k:
            hg[k].wait_recv()
        to = mod(z - k - y, 8)
        total = None
        for b in range(NB):
            term = jnp.dot(hid[k, :, pl.ds(HB * b, HB)], wd[mod(b - z_hi, 4)], preferred_element_type=F32)
            total = term if total is None else total + term
        ry_send[to] = total.astype(BF16)

        @pl.when(to != 0)
        def _(to=to):
            ry(to).start()

    for k in near_first:
        ry(k).wait_recv()
    for i in range(8):
        cols = pl.ds(HD * i, HD)
        feed = ry_send[0, :, cols].astype(F32)
        for k in range(1, 8):
            feed = feed + ry_recv[k, :, cols].astype(F32)
        relay[pl.ds(i, ROWS, stride=8), :] = feed
    f_send[...] = relay[...].astype(BF16).reshape(N, ROWS, HD)

    me = tile_of(z)
    a2 = [
        remote(f_send.at[mod(z + k, 8)], f_recv.at[me], a2_ssem.at[k - 1], a2_rsem.at[k - 1], at_z(k)) for k in far_first
    ]
    for copy in a2:
        copy.start()
    f_recv[me] = f_send[z]
    for copy in a2:
        copy.wait_recv()
    for e in range(N):
        mix = jnp.concatenate([mixed[pl.ds(QH * r + 8 * e, 8), :] for r in range(R)], 0)
        natural[pl.ds(ROWS * e, ROWS), :] = mix + f_recv[e].astype(F32)
    for e in range(N):
        for i in range(8):
            out_ref[:, pl.ds(FB * e + HD * i, HD)] = natural[pl.ds(ROWS * e + i, R, stride=8), :].astype(BF16)

    for copy in a1 + a2 + list(ag.values()) + list(hg.values()):
        copy.wait_send()
    for k in far_first:
        rz(k).wait_send()
        ry(k).wait_send()

    @pl.when(c == 0)
    def _():
        for k in (1, 2, 3):
            for i in range(3):
                weight_z(k, i).wait_send()
            for to in (1, 2, 3):
                for i in range(2):
                    weight_x(k, to, i).wait_send()
        for i in range(2):
            weight_c(i).wait_send()


def per_device(q, ck, cv, nk, nv, lengths, residual, gain, gate, up, down):
    vmem = pl.BlockSpec(memory_space=pltpu.VMEM)
    smem = pl.BlockSpec(memory_space=pltpu.SMEM)
    hbm = pl.BlockSpec(memory_space=pl.ANY)
    dma = pltpu.SemaphoreType.DMA
    return pl.pallas_call(
        kernel,
        out_shape=jax.ShapeDtypeStruct((R, QH * HD), BF16),
        in_specs=[smem] + [hbm] * 10,
        out_specs=vmem,
        scratch_shapes=[
            pltpu.VMEM((R, QH, HD), BF16),
            pltpu.VMEM((R, L, KVH * HD), BF16),
            pltpu.VMEM((R, L, KVH * HD), BF16),
            pltpu.VMEM((R, KVH * HD), BF16),
            pltpu.VMEM((R, KVH * HD), BF16),
            pltpu.VMEM((R, QH * HD), BF16),
            pltpu.VMEM((QH, HD), F32),
            pltpu.VMEM((NB, FB, 2 * HB), BF16),
            pltpu.VMEM((NB, HB, FB), BF16),
            pltpu.VMEM((R * QH, L), F32),
            pltpu.VMEM((R * QH, HD), F32),
            pltpu.VMEM((R * QH, HD), F32),
            pltpu.VMEM((N, ROWS, HD), BF16),
            pltpu.VMEM((N, ROWS, HD), BF16),
            pltpu.VMEM((N * ROWS, HD), F32),
            pltpu.VMEM((N, ROWS, FB), BF16),
            pltpu.VMEM((N, ROWS, FB), BF16),
            pltpu.VMEM((N, ROWS, FB), BF16),
            pltpu.VMEM((N, ROWS, NB * HB), BF16),
            pltpu.VMEM((N, ROWS, FB), BF16),
            pltpu.VMEM((N, ROWS, FB), BF16),
            pltpu.VMEM((N, ROWS, HD), BF16),
            pltpu.VMEM((N, ROWS, HD), BF16),
            dma((7,)), dma((3,)),
            dma((3, 3)), dma((3, 3)),
            dma((3, 3, 2)), dma((3, 3, 2)),
            dma((2,)), dma((2,)),
            pltpu.SemaphoreType.REGULAR,
            dma((7,)), dma((7,)),
            dma((7,)), dma((7,)),
            dma((8,)), dma((8,)),
            dma((7,)), dma((7,)),
            dma((8,)), dma((8,)),
            dma((7,)), dma((7,)),
        ],
        compiler_params=pltpu.CompilerParams(
            collective_id=0, has_side_effects=True, vmem_limit_bytes=60 * 1024 * 1024
        ),
        cost_estimate=pl.CostEstimate(flops=1_400_000_000, bytes_accessed=5_000_000, transcendentals=100_000),
    )(lengths, q, ck, cv, nk, nv, residual, gain.reshape(QH, HD), gate, up, down)


def solution(mesh):
    rows = ("pair", "role", "shard")
    return jax.shard_map(
        per_device,
        mesh=mesh,
        in_specs=(
            P(rows, None, None), P(rows, None, None), P(rows, None, None), P(rows, None), P(rows, None), P(rows),
            P(rows, None), P(), P("role", "shard"), P("role", "shard"), P("shard", "role"),
        ),
        out_specs=P(rows, None),
        check_vma=False,
    )
```

time: 108 us -> 103 us (0.954)
  the two profiles are of different devices: /device:TPU:8 before, /device:TPU:4 now
where the time goes in v2:
time: 103 us
  Pallas kernels  101 us (98%)
  local copies, waits for them, and re-layouts  1.57 us (2%)
    pallas_call x1, Pallas kernels, per_device(): pl.pallas_call(kernel, out_shape=jax.ShapeDtypeStruct((R, QH * HD), BF16)...  101 us

profile of v2, /device:TPU:4, one launch (start us, length us, event | category | flops | bytes accessed | tf_op | source)
XLA Modules:
  0.0 102.6 jit_solution(9060234284089152151)
XLA Ops:
  0.0 101.0 %shard_map.109 = bf16[6,8192]{1,0:T(8,128)(2,1)} custom-call(s32[6]{0:T(128)} %len_ref.1, bf16[6,64,128]{2,1,0:T(8,128)(2,1)} %q_hbm.1, bf16[6,128,512]{2,1,0:T(8,128)(2,1)} %ck_hbm.1, bf16[6,128,512]{2,1,0:T(8,128)(2,1)} %cv_hbm.1, bf16[6,512]{1,0:T(8,128)(2,1)} %nk_hbm.1, bf16[6,512]{1,0:T(8,128)(2,1)} %nv_hbm.1, bf16[6,8192]{1,0:T(8,128)(2,1)} %res_hbm.1, ...), custom_call_target="tpu_custom_call" | custom-call | flops 1400000000 | bytes 5000000 | tf_op jit(solution)/shard_map/pallas_call | solution.py:340
  101.1 1.6 %copy.13 = bf16[6,8192]{1,0:T(8,128)(2,1)} copy(bf16[6,8192]{1,0:T(8,128)(2,1)} %shard_map.109) | data formatting | bytes 196608

commit v3 on v2

--- a/solution.py
+++ b/solution.py
@@ -30,7 +30,7 @@
     len_ref, q_hbm, ck_hbm, cv_hbm, nk_hbm, nv_hbm, res_hbm, gain_hbm, gate_hbm, up_hbm, down_hbm,
     out_ref,
     q_ref, ck, cv, nk_ref, nv_ref, res_ref, gain_ref, wgu, wd, scores, mixed, natural, n_send, n_recv, relay,
-    acts, rz_send, rz_recv, hid, ry_send, ry_recv, f_send, f_recv,
+    acts, terms, rz_send, rz_recv, hid, ry_send, ry_recv, f_send, f_recv,
     local_sem, own_sem, wz_ssem, wz_rsem, wx_ssem, wx_rsem, wc_ssem, wc_rsem, ready_sem, a1_ssem, a1_rsem, ag_ssem, ag_rsem,
     rz_ssem, rz_rsem, hg_ssem, hg_rsem, ry_ssem, ry_rsem, a2_ssem, a2_rsem,
 ):
@@ -81,6 +81,7 @@
 
     for k in range(1, 8):
         greet(at_z(k))
+    for k in (1, 2, 6, 7):
         greet(at_y(k))
 
     @pl.when(c == 0)
@@ -88,11 +89,11 @@
         for k in range(1, 4):
             greet(at_x(k))
         greet(sibling)
-        pl.semaphore_wait(barrier, 17)
+        pl.semaphore_wait(barrier, 14)
 
     @pl.when(c == 1)
     def _():
-        pl.semaphore_wait(barrier, 15)
+        pl.semaphore_wait(barrier, 12)
         pl.semaphore_signal(ready_sem, inc=1, device_id=sibling, device_id_type=MESH)
 
     part = pl.ds(pl.multiple_of(x * 256, 256), 256)
@@ -119,17 +120,9 @@
 
     @pl.when(c == 0)
     def _():
-        for k in (1, 3, 2):
+        for k in (1, 3):
             weight_z(k, 0).start()
             weight_z(k, 1).start()
-
-    def pass_gate_up(k):
-        @pl.when(c == 0)
-        def _():
-            weight_z(k, 0).wait_recv()
-            weight_z(k, 1).wait_recv()
-            for to in (2, 1, 3):
-                weight_x(k, to, 0).start()
 
     for copy in operands[:2]:
         copy.wait()
@@ -146,8 +139,6 @@
     scale = F32(1.0) / jnp.sqrt(F32(HD))
     slot = lax.broadcasted_iota(jnp.int32, (QH, L), 1)
     for r in range(R):
-        if r in (2, 3, 4):
-            pass_gate_up((1, 3, 2)[r - 2])
         rows = pl.ds(QH * r, QH)
         keys = [jnp.broadcast_to(nk_ref[pl.ds(r, 1), pl.ds(HD * k, HD)].astype(F32), (GRP, HD)) for k in range(KVH)]
         vals = [jnp.broadcast_to(nv_ref[pl.ds(r, 1), pl.ds(HD * k, HD)].astype(F32), (GRP, HD)) for k in range(KVH)]
@@ -178,7 +169,6 @@
         return lax.rem(at, 2) * 4 + at // 2
 
     far_first = (4, 3, 5, 2, 6, 1, 7)
-    near_first = (1, 7, 2, 6, 3, 5, 4)
     a1 = [
         remote(n_send.at[tile_of(mod(z + k, 8))], n_recv.at[z], a1_ssem.at[k - 1], a1_rsem.at[k - 1], at_z(k))
         for k in far_first
@@ -189,113 +179,175 @@
 
     @pl.when(c == 0)
     def _():
-        for k in (1, 3, 2):
-            weight_z(k, 2).start()
+        weight_z(2, 0).start()
+        weight_z(2, 1).start()
+        for k in (1, 3):
+            weight_z(k, 0).wait_recv()
+            weight_z(k, 1).wait_recv()
+            for to in (2, 1, 3):
+                weight_x(k, to, 0).start()
 
     for copy in a1:
         copy.wait_recv()
     relay[...] = n_recv[...].reshape(N * ROWS, HD).astype(F32)
     acts[0] = jnp.concatenate([relay[pl.ds(i, ROWS, stride=8), :] for i in range(8)], 1).astype(BF16)
 
-    ag = {k: remote(acts.at[0], acts.at[k], ag_ssem.at[k - 1], ag_rsem.at[k - 1], at_y(k)) for k in far_first}
-    for k in far_first:
-        ag[k].start()
-
-    @pl.when(c == 0)
-    def _():
-        for k in (1, 3, 2):
-            weight_z(k, 2).wait_recv()
+    sent = []
+
+    def push(*args):
+        copy = remote(*args)
+        copy.start()
+        sent.append(copy)
+        return copy
+
+    def gather(buf, at, ssem, rsem, width, visit, begun):
+        half = width // 2
+        cols = [pl.ds(0, half), pl.ds(half, half)]
+        two = {}
+        for i in range(2):
+            for way, k in enumerate((2, 6)):
+                s = i if way == 0 else 1 - i
+                n = 2 * way + s
+                two[way, s] = push(buf.at[0, :, cols[s]], buf.at[k, :, cols[s]], ssem.at[n], rsem.at[n], at(k))
+        one = [push(buf.at[0], buf.at[k], ssem.at[4 + n], rsem.at[4 + n], at(k)) for n, k in enumerate((1, 7))]
+        begun()
+        four, three = [], {}
+        for i in range(2):
+            for way, k in enumerate((2, 6)):
+                s = i if way == 0 else 1 - i
+                two[way, s].wait_recv()
+                if i == 0:
+                    n = 6 + way
+                    four.append(push(buf.at[k, :, cols[s]], buf.at[4, :, cols[s]], ssem.at[n], rsem.at[n], at(k)))
+                n = 8 + 2 * way + s
+                to, place = ((1, 3), (7, 5))[way]
+                three[way, s] = push(buf.at[k, :, cols[s]], buf.at[place, :, cols[s]], ssem.at[n], rsem.at[n], at(to))
+        visit((0, 2, 6))
+        for copy in one:
+            copy.wait_recv()
+        visit((1, 7))
+        for copy in list(three.values()) + four:
+            copy.wait_recv()
+        visit((3, 5, 4))
+
+    def scatter(term, at, ssem, rsem, sbuf, rbuf):
+        cols = [pl.ds(0, HALF), pl.ds(HALF, HALF)]
+
+        def send(value, place, s, n, k):
+            sbuf[place, :, cols[s]] = value.astype(BF16)
+            ref = sbuf.at[place, :, cols[s]]
+            return push(ref, rbuf.at[place, :, cols[s]], ssem.at[n], rsem.at[n], at(k))
+
+        four = [send(term(4, s), 4, s, s, (2, 6)[s]) for s in range(2)]
+        three = {}
+        for i in range(2):
+            for way in range(2):
+                s = 1 - i if way == 0 else i
+                three[way, s] = send(term((3, 5)[way], s), (3, 5)[way], s, 2 + 2 * way + s, (1, 7)[way])
+        one = [send(term(k, s), k, s, 6 + 2 * way + s, k) for way, k in enumerate((1, 7)) for s in range(2)]
+        two = []
+        for i in range(2):
+            for way, k in enumerate((2, 6)):
+                s = 1 - i if way == 0 else i
+                value = term(k, s)
+                three[way, s].wait_recv()
+                value = value + rbuf[(3, 5)[way], :, cols[s]].astype(F32)
+                if i == 1:
+                    four[s].wait_recv()
+                    value = value + rbuf[4, :, cols[s]].astype(F32)
+                two.append(send(value, k, s, 10 + 2 * way + s, k))
+        for copy in one + two:
+            copy.wait_recv()
+        out = []
+        for s in range(2):
+            value = term(0, s)
+            for k in (1, 7, 2, 6):
+                value = value + rbuf[k, :, cols[s]].astype(F32)
+            out.append(value)
+        return out
+
+    def weights_begun():
+        @pl.when(c == 0)
+        def _():
+            for k in (1, 3, 2):
+                weight_z(k, 2).start()
+            weight_z(2, 0).wait_recv()
+            weight_z(2, 1).wait_recv()
             for to in (2, 1, 3):
-                weight_x(k, to, 1).start()
-        for k in (1, 3, 2):
-            for to in (2, 1, 3):
-                weight_x(k, to, 0).wait_recv()
-
-    @pl.when(c == 1)
-    def _():
-        weight_c(0).wait_recv()
-
-    own[0].wait()
-    own[1].wait()
-
-    def rz(k):
-        return remote(rz_send.at[k], rz_recv.at[k], rz_ssem.at[k], rz_rsem.at[k], at_z(k))
-
-    for n, k in enumerate((0,) + near_first):
-        if k:
-            ag[k].wait_recv()
-        to = mod(y - k - z, 8)
-        rows = acts[k]
-        for b in range(NB):
-            rz_send[to, :, pl.ds(2 * HB * b, 2 * HB)] = jnp.dot(
-                rows, wgu[mod(b - z_hi, 4)], preferred_element_type=F32
-            ).astype(BF16)
-
-        @pl.when(to != 0)
-        def _(to=to):
-            rz(to).start()
-
-        if n == 4:
+                weight_x(2, to, 0).start()
+
+    def gate_up(places):
+        if 0 in places:
+            own[0].wait()
+            own[1].wait()
+
             @pl.when(c == 0)
             def _():
-                pl.semaphore_wait(ready_sem, 1)
-                weight_c(0).start()
-
-    for k in near_first:
-        rz(k).wait_recv()
+                for k in (1, 3, 2):
+                    weight_z(k, 2).wait_recv()
+                    for to in (2, 1, 3):
+                        weight_x(k, to, 1).start()
+                for k in (1, 3, 2):
+                    for to in (2, 1, 3):
+                        weight_x(k, to, 0).wait_recv()
+
+            @pl.when(c == 1)
+            def _():
+                weight_c(0).wait_recv()
+
+        rows = jnp.concatenate([acts[k] for k in places], 0)
+        for b in range(NB):
+            sums = jnp.dot(rows, wgu[mod(b - z_hi, 4)], preferred_element_type=F32)
+            for n, k in enumerate(places):
+                terms[k, :, pl.ds(2 * HB * b, 2 * HB)] = sums[ROWS * n:ROWS * (n + 1)]
+
+    gather(acts, at_y, ag_ssem, ag_rsem, FB, gate_up, weights_begun)
+
+    @pl.when(c == 0)
+    def _():
+        pl.semaphore_wait(ready_sem, 1)
+        weight_c(0).start()
+
+    def for_z(k, s):
+        return terms[mod(y - z - k, 8), :, pl.ds(s * HALF, HALF)]
+
+    both = scatter(for_z, at_z, rz_ssem, rz_rsem, rz_send, rz_recv)
     for b in range(NB):
-        cols = pl.ds(2 * HB * b, 2 * HB)
-        both = rz_send[0, :, cols].astype(F32)
-        for k in range(1, 8):
-            both = both + rz_recv[k, :, cols].astype(F32)
-        gate, up = both[:, :HB], both[:, HB:]
+        gate = both[b // 2][:, 2 * HB * (b % 2):2 * HB * (b % 2) + HB]
+        up = both[b // 2][:, 2 * HB * (b % 2) + HB:2 * HB * (b % 2 + 1)]
         hid[0, :, pl.ds(HB * b, HB)] = (gate / (F32(1.0) + jnp.exp(-gate)) * up).astype(BF16)
 
-    hg = {k: remote(hid.at[0], hid.at[k], hg_ssem.at[k - 1], hg_rsem.at[k - 1], at_z(k)) for k in far_first}
-    for k in far_first:
-        hg[k].start()
-
-    @pl.when(c == 0)
-    def _():
-        for k in (1, 3, 2):
-            for to in (2, 1, 3):
-                weight_x(k, to, 1).wait_recv()
-
-    own[2].wait()
-
-    @pl.when(c == 0)
-    def _():
-        weight_c(1).start()
-
-    @pl.when(c == 1)
-    def _():
-        weight_c(1).wait_recv()
-
-    def ry(k):
-        return remote(ry_send.at[k], ry_recv.at[k], ry_ssem.at[k], ry_rsem.at[k], at_y(k))
-
-    for k in (0,) + near_first:
-        if k:
-            hg[k].wait_recv()
-        to = mod(z - k - y, 8)
+    def down(places):
+        if 0 in places:
+            own[2].wait()
+
+            @pl.when(c == 0)
+            def _():
+                for k in (1, 3, 2):
+                    for to in (2, 1, 3):
+                        weight_x(k, to, 1).wait_recv()
+                weight_c(1).start()
+
+            @pl.when(c == 1)
+            def _():
+                weight_c(1).wait_recv()
+
+        rows = jnp.concatenate([hid[k] for k in places], 0)
         total = None
         for b in range(NB):
-            term = jnp.dot(hid[k, :, pl.ds(HB * b, HB)], wd[mod(b - z_hi, 4)], preferred_element_type=F32)
+            term = jnp.dot(rows[:, HB * b:HB * (b + 1)], wd[mod(b - z_hi, 4)], preferred_element_type=F32)
             total = term if total is None else total + term
-        ry_send[to] = total.astype(BF16)
-
-        @pl.when(to != 0)
-        def _(to=to):
-            ry(to).start()
-
-    for k in near_first:
-        ry(k).wait_recv()
+        for n, k in enumerate(places):
+            terms[k] = total[ROWS * n:ROWS * (n + 1)]
+
+    gather(hid, at_z, hg_ssem, hg_rsem, NB * HB, down, lambda: None)
+
+    def for_y(k, s):
+        return terms[mod(z - y - k, 8), :, pl.ds(s * HALF, HALF)]
+
+    feed = scatter(for_y, at_y, ry_ssem, ry_rsem, ry_send, ry_recv)
     for i in range(8):
-        cols = pl.ds(HD * i, HD)
-        feed = ry_send[0, :, cols].astype(F32)
-        for k in range(1, 8):
-            feed = feed + ry_recv[k, :, cols].astype(F32)
-        relay[pl.ds(i, ROWS, stride=8), :] = feed
+        relay[pl.ds(i, ROWS, stride=8), :] = feed[i // 4][:, HD * (i % 4):HD * (i % 4 + 1)]
     f_send[...] = relay[...].astype(BF16).reshape(N, ROWS, HD)
 
     me = tile_of(z)
@@ -314,11 +366,8 @@
         for i in range(8):
             out_ref[:, pl.ds(FB * e + HD * i, HD)] = natural[pl.ds(ROWS * e + i, R, stride=8), :].astype(BF16)
 
-    for copy in a1 + a2 + list(ag.values()) + list(hg.values()):
+    for copy in a1 + a2 + sent:
         copy.wait_send()
-    for k in far_first:
-        rz(k).wait_send()
-        ry(k).wait_send()
 
     @pl.when(c == 0)
     def _():
@@ -359,6 +408,7 @@
             pltpu.VMEM((N, ROWS, HD), BF16),
             pltpu.VMEM((N * ROWS, HD), F32),
             pltpu.VMEM((N, ROWS, FB), BF16),
+            pltpu.VMEM((N, ROWS, FB), F32),
             pltpu.VMEM((N, ROWS, FB), BF16),
             pltpu.VMEM((N, ROWS, FB), BF16),
             pltpu.VMEM((N, ROWS, NB * HB), BF16),
@@ -372,10 +422,10 @@
             dma((2,)), dma((2,)),
             pltpu.SemaphoreType.REGULAR,
             dma((7,)), dma((7,)),
-            dma((7,)), dma((7,)),
-            dma((8,)), dma((8,)),
-            dma((7,)), dma((7,)),
-            dma((8,)), dma((8,)),
+            dma((12,)), dma((12,)),
+            dma((14,)), dma((14,)),
+            dma((12,)), dma((12,)),
+            dma((14,)), dma((14,)),
             dma((7,)), dma((7,)),
         ],
         compiler_params=pltpu.CompilerParams(

time: 103 us -> 78.9 us (0.77)
  the two profiles are of different devices: /device:TPU:4 before, /device:TPU:1 now
where the time goes in v3:
time: 78.9 us; the launch traced here: 78.8 us
  Pallas kernels  77.2 us (98%)
  local copies, waits for them, and re-layouts  1.57 us (2%)
    pallas_call x1, Pallas kernels, per_device(): pl.pallas_call(kernel, out_shape=jax.ShapeDtypeStruct((R, QH * HD), BF16)...  77.2 us

profile of v3, /device:TPU:1, one launch (start us, length us, event | category | flops | bytes accessed | tf_op | source)
XLA Modules:
  0.0 78.8 jit_solution(8766789155123394786)
XLA Ops:
  0.0 77.2 %shard_map.109 = bf16[6,8192]{1,0:T(8,128)(2,1)} custom-call(s32[6]{0:T(128)} %len_ref.1, bf16[6,64,128]{2,1,0:T(8,128)(2,1)} %q_hbm.1, bf16[6,128,512]{2,1,0:T(8,128)(2,1)} %ck_hbm.1, bf16[6,128,512]{2,1,0:T(8,128)(2,1)} %cv_hbm.1, bf16[6,512]{1,0:T(8,128)(2,1)} %nk_hbm.1, bf16[6,512]{1,0:T(8,128)(2,1)} %nv_hbm.1, bf16[6,8192]{1,0:T(8,128)(2,1)} %res_hbm.1, ...), custom_call_target="tpu_custom_call" | custom-call | flops 1400000000 | bytes 5000000 | tf_op jit(solution)/shard_map/pallas_call | solution.py:389
  77.2 1.6 %copy.13 = bf16[6,8192]{1,0:T(8,128)(2,1)} copy(bf16[6,8192]{1,0:T(8,128)(2,1)} %shard_map.109) | data formatting | bytes 196608

commit v4 on v3

--- a/solution.py
+++ b/solution.py
@@ -27,11 +27,11 @@
 
 
 def kernel(
-    len_ref, q_hbm, ck_hbm, cv_hbm, nk_hbm, nv_hbm, res_hbm, gain_hbm, gate_hbm, up_hbm, down_hbm,
+    len_hbm, q_hbm, ck_hbm, cv_hbm, nk_hbm, nv_hbm, res_hbm, gain_hbm, gate_hbm, up_hbm, down_hbm,
     out_ref,
-    q_ref, ck, cv, nk_ref, nv_ref, res_ref, gain_ref, wgu, wd, scores, mixed, natural, n_send, n_recv, relay,
+    len_ref, q_ref, ck, cv, nk_ref, nv_ref, res_ref, gain_ref, wgu, wd, scores, mixed, natural, n_send, n_recv, relay,
     acts, terms, rz_send, rz_recv, hid, ry_send, ry_recv, f_send, f_recv,
-    local_sem, own_sem, wz_ssem, wz_rsem, wx_ssem, wx_rsem, wc_ssem, wc_rsem, ready_sem, a1_ssem, a1_rsem, ag_ssem, ag_rsem,
+    local_sem, own_sem, wz_ssem, wz_rsem, wx_ssem, wx_rsem, wc_ssem, wc_rsem, a1_ssem, a1_rsem, ag_ssem, ag_rsem,
     rz_ssem, rz_rsem, hg_ssem, hg_rsem, ry_ssem, ry_rsem, a2_ssem, a2_rsem,
 ):
     pair, role, shard = lax.axis_index("pair"), lax.axis_index("role"), lax.axis_index("shard")
@@ -58,7 +58,7 @@
 
     operands = []
     for i, (src, dst) in enumerate((
-        (q_hbm, q_ref), (ck_hbm, ck), (cv_hbm, cv), (nk_hbm, nk_ref), (nv_hbm, nv_ref), (res_hbm, res_ref), (gain_hbm, gain_ref),
+        (q_hbm, q_ref), (ck_hbm, ck), (len_hbm, len_ref), (cv_hbm, cv), (nk_hbm, nk_ref), (nv_hbm, nv_ref), (res_hbm, res_ref), (gain_hbm, gain_ref),
     )):
         copy = pltpu.make_async_copy(src, dst, local_sem.at[i])
         copy.start()
@@ -84,24 +84,18 @@
     for k in (1, 2, 6, 7):
         greet(at_y(k))
 
-    @pl.when(c == 0)
-    def _():
-        for k in range(1, 4):
-            greet(at_x(k))
-        greet(sibling)
-        pl.semaphore_wait(barrier, 14)
-
-    @pl.when(c == 1)
-    def _():
-        pl.semaphore_wait(barrier, 12)
-        pl.semaphore_signal(ready_sem, inc=1, device_id=sibling, device_id_type=MESH)
-
-    part = pl.ds(pl.multiple_of(x * 256, 256), 256)
-    part_d = pl.ds(pl.multiple_of(x * 32, 32), 32)
+    for k in range(1, 4):
+        greet(at_x(k))
+    greet(sibling)
+    pl.semaphore_wait(barrier, 15)
+
+    p = c * 4 + x
+    part = pl.ds(pl.multiple_of(p * 128, 128), 128)
+    part_d = pl.ds(pl.multiple_of(p * 16, 16), 16)
 
     def weight_z(k, i):
         q_to = mod(z_hi + k, 4)
-        rows = pl.ds(pl.multiple_of(q_to * FB + x * 256, 256), 256)
+        rows = pl.ds(pl.multiple_of(q_to * FB + p * 128, 128), 128)
         cols = pl.ds(pl.multiple_of(q_to * FB, FB), FB)
         src, dst = (
             (gate_hbm.at[rows, :], wgu.at[4 - k, part, pl.ds(0, HB)]),
@@ -114,15 +108,16 @@
         ref = (wgu.at[4 - k, part, :], wd.at[4 - k, part_d, :])[i]
         return remote(ref, ref, wx_ssem.at[k - 1, to - 1, i], wx_rsem.at[k - 1, to - 1, i], at_x(to))
 
-    def weight_c(i):
-        ref = (wgu, wd)[i].at[pl.ds(1, 3)]
-        return remote(ref, ref, wc_ssem.at[i], wc_rsem.at[i], sibling)
-
-    @pl.when(c == 0)
-    def _():
-        for k in (1, 3):
-            weight_z(k, 0).start()
-            weight_z(k, 1).start()
+    for k in (1, 3):
+        weight_z(k, 0).start()
+        weight_z(k, 1).start()
+
+    def weight_c(k, i):
+        ref = (
+            wgu.at[4 - k, pl.ds(pl.multiple_of(c * 512, 512), 512), :],
+            wd.at[4 - k, pl.ds(pl.multiple_of(c * 64, 64), 64), :],
+        )[i]
+        return remote(ref, ref, wc_ssem.at[k - 1, i], wc_rsem.at[k - 1, i], sibling)
 
     for copy in operands[:2]:
         copy.wait()
@@ -177,15 +172,13 @@
         copy.start()
     n_recv[z] = n_send[tile_of(z)]
 
-    @pl.when(c == 0)
-    def _():
-        weight_z(2, 0).start()
-        weight_z(2, 1).start()
-        for k in (1, 3):
-            weight_z(k, 0).wait_recv()
-            weight_z(k, 1).wait_recv()
-            for to in (2, 1, 3):
-                weight_x(k, to, 0).start()
+    weight_z(2, 0).start()
+    weight_z(2, 1).start()
+    for k in (1, 3):
+        weight_z(k, 0).wait_recv()
+        weight_z(k, 1).wait_recv()
+        for to in (2, 1, 3):
+            weight_x(k, to, 0).start()
 
     for copy in a1:
         copy.wait_recv()
@@ -267,33 +260,28 @@
         return out
 
     def weights_begun():
-        @pl.when(c == 0)
-        def _():
-            for k in (1, 3, 2):
-                weight_z(k, 2).start()
-            weight_z(2, 0).wait_recv()
-            weight_z(2, 1).wait_recv()
-            for to in (2, 1, 3):
-                weight_x(2, to, 0).start()
+        for k in (1, 3, 2):
+            weight_z(k, 2).start()
+        weight_z(2, 0).wait_recv()
+        weight_z(2, 1).wait_recv()
+        for to in (2, 1, 3):
+            weight_x(2, to, 0).start()
 
     def gate_up(places):
         if 0 in places:
             own[0].wait()
             own[1].wait()
 
-            @pl.when(c == 0)
-            def _():
-                for k in (1, 3, 2):
-                    weight_z(k, 2).wait_recv()
-                    for to in (2, 1, 3):
-                        weight_x(k, to, 1).start()
-                for k in (1, 3, 2):
-                    for to in (2, 1, 3):
-                        weight_x(k, to, 0).wait_recv()
-
-            @pl.when(c == 1)
-            def _():
-                weight_c(0).wait_recv()
+            for k in (1, 3, 2):
+                for to in (1, 3, 2):
+                    weight_x(k, to, 0).wait_recv()
+                weight_c(k, 0).start()
+            for k in (1, 3, 2):
+                weight_z(k, 2).wait_recv()
+                for to in (2, 1, 3):
+                    weight_x(k, to, 1).start()
+            for k in (1, 3, 2):
+                weight_c(k, 0).wait_recv()
 
         rows = jnp.concatenate([acts[k] for k in places], 0)
         for b in range(NB):
@@ -303,11 +291,6 @@
 
     gather(acts, at_y, ag_ssem, ag_rsem, FB, gate_up, weights_begun)
 
-    @pl.when(c == 0)
-    def _():
-        pl.semaphore_wait(ready_sem, 1)
-        weight_c(0).start()
-
     def for_z(k, s):
         return terms[mod(y - z - k, 8), :, pl.ds(s * HALF, HALF)]
 
@@ -321,16 +304,8 @@
         if 0 in places:
             own[2].wait()
 
-            @pl.when(c == 0)
-            def _():
-                for k in (1, 3, 2):
-                    for to in (2, 1, 3):
-                        weight_x(k, to, 1).wait_recv()
-                weight_c(1).start()
-
-            @pl.when(c == 1)
-            def _():
-                weight_c(1).wait_recv()
+            for k in (1, 3, 2):
+                weight_c(k, 1).wait_recv()
 
         rows = jnp.concatenate([hid[k] for k in places], 0)
         total = None
@@ -340,7 +315,13 @@
         for n, k in enumerate(places):
             terms[k] = total[ROWS * n:ROWS * (n + 1)]
 
-    gather(hid, at_z, hg_ssem, hg_rsem, NB * HB, down, lambda: None)
+    def hand_down():
+        for k in (1, 3, 2):
+            for to in (1, 3, 2):
+                weight_x(k, to, 1).wait_recv()
+            weight_c(k, 1).start()
+
+    gather(hid, at_z, hg_ssem, hg_rsem, NB * HB, down, hand_down)
 
     def for_y(k, s):
         return terms[mod(z - y - k, 8), :, pl.ds(s * HALF, HALF)]
@@ -369,29 +350,27 @@
     for copy in a1 + a2 + sent:
         copy.wait_send()
 
-    @pl.when(c == 0)
-    def _():
-        for k in (1, 2, 3):
-            for i in range(3):
-                weight_z(k, i).wait_send()
-            for to in (1, 2, 3):
-                for i in range(2):
-                    weight_x(k, to, i).wait_send()
+    for k in (1, 2, 3):
+        for i in range(3):
+            weight_z(k, i).wait_send()
+        for to in (1, 2, 3):
+            for i in range(2):
+                weight_x(k, to, i).wait_send()
         for i in range(2):
-            weight_c(i).wait_send()
+            weight_c(k, i).wait_send()
 
 
 def per_device(q, ck, cv, nk, nv, lengths, residual, gain, gate, up, down):
     vmem = pl.BlockSpec(memory_space=pltpu.VMEM)
-    smem = pl.BlockSpec(memory_space=pltpu.SMEM)
     hbm = pl.BlockSpec(memory_space=pl.ANY)
     dma = pltpu.SemaphoreType.DMA
     return pl.pallas_call(
         kernel,
         out_shape=jax.ShapeDtypeStruct((R, QH * HD), BF16),
-        in_specs=[smem] + [hbm] * 10,
+        in_specs=[hbm] * 11,
         out_specs=vmem,
         scratch_shapes=[
+            pltpu.SMEM((R,), jnp.int32),
             pltpu.VMEM((R, QH, HD), BF16),
             pltpu.VMEM((R, L, KVH * HD), BF16),
             pltpu.VMEM((R, L, KVH * HD), BF16),
@@ -416,11 +395,10 @@
             pltpu.VMEM((N, ROWS, FB), BF16),
             pltpu.VMEM((N, ROWS, HD), BF16),
             pltpu.VMEM((N, ROWS, HD), BF16),
-            dma((7,)), dma((3,)),
+            dma((8,)), dma((3,)),
             dma((3, 3)), dma((3, 3)),
             dma((3, 3, 2)), dma((3, 3, 2)),
-            dma((2,)), dma((2,)),
-            pltpu.SemaphoreType.REGULAR,
+            dma((3, 2)), dma((3, 2)),
             dma((7,)), dma((7,)),
             dma((12,)), dma((12,)),
             dma((14,)), dma((14,)),

time: 78.9 us -> 77.1 us (0.977)
  the two profiles are of different devices: /device:TPU:1 before, /device:TPU:4 now
where the time goes in v4:
time: 77.1 us; the launch traced here: 77 us
  Pallas kernels  75.4 us (98%)
  local copies, waits for them, and re-layouts  1.57 us (2%)
    pallas_call x1, Pallas kernels, per_device(): pl.pallas_call(kernel, out_shape=jax.ShapeDtypeStruct((R, QH * HD), BF16)...  75.4 us
    unnamed x1, local copies, waits for them, and re-layouts  1.57 us

profile of v4, /device:TPU:4, one launch (start us, length us, event | category | flops | bytes accessed | tf_op | source)
XLA Modules:
  0.0 77.0 jit_solution(17320137676348643168)
XLA Ops:
  0.0 75.4 %shard_map.109 = bf16[6,8192]{1,0:T(8,128)(2,1)} custom-call(s32[6]{0:T(128)} %len_hbm.1, bf16[6,64,128]{2,1,0:T(8,128)(2,1)} %q_hbm.1, bf16[6,128,512]{2,1,0:T(8,128)(2,1)} %ck_hbm.1, bf16[6,128,512]{2,1,0:T(8,128)(2,1)} %cv_hbm.1, bf16[6,512]{1,0:T(8,128)(2,1)} %nk_hbm.1, bf16[6,512]{1,0:T(8,128)(2,1)} %nv_hbm.1, bf16[6,8192]{1,0:T(8,128)(2,1)} %res_hbm.1, ...), custom_call_target="tpu_custom_call" | custom-call | flops 1400000000 | bytes 5000000 | tf_op jit(solution)/shard_map/pallas_call | solution.py:367
  75.4 1.6 %copy.13 = bf16[6,8192]{1,0:T(8,128)(2,1)} copy(bf16[6,8192]{1,0:T(8,128)(2,1)} %shard_map.109) | data formatting | bytes 196608

commit v5 on v4

--- a/solution.py
+++ b/solution.py
@@ -91,7 +91,7 @@
 
     p = c * 4 + x
     part = pl.ds(pl.multiple_of(p * 128, 128), 128)
-    part_d = pl.ds(pl.multiple_of(p * 16, 16), 16)
+    part_d = pl.ds(pl.multiple_of(x * 32, 32), 32)
 
     def weight_z(k, i):
         q_to = mod(z_hi + k, 4)
@@ -115,7 +115,7 @@
     def weight_c(k, i):
         ref = (
             wgu.at[4 - k, pl.ds(pl.multiple_of(c * 512, 512), 512), :],
-            wd.at[4 - k, pl.ds(pl.multiple_of(c * 64, 64), 64), :],
+            wd.at[4 - k],
         )[i]
         return remote(ref, ref, wc_ssem.at[k - 1, i], wc_rsem.at[k - 1, i], sibling)
 
@@ -259,9 +259,20 @@
             out.append(value)
         return out
 
+    def down_along():
+        @pl.when(c == 1)
+        def _():
+            for k in (1, 3, 2):
+                weight_z(k, 2).wait_recv()
+                for to in (2, 1, 3):
+                    weight_x(k, to, 1).start()
+
     def weights_begun():
-        for k in (1, 3, 2):
-            weight_z(k, 2).start()
+        @pl.when(c == 1)
+        def _():
+            for k in (1, 3, 2):
+                weight_z(k, 2).start()
+
         weight_z(2, 0).wait_recv()
         weight_z(2, 1).wait_recv()
         for to in (2, 1, 3):
@@ -276,18 +287,17 @@
                 for to in (1, 3, 2):
                     weight_x(k, to, 0).wait_recv()
                 weight_c(k, 0).start()
-            for k in (1, 3, 2):
-                weight_z(k, 2).wait_recv()
-                for to in (2, 1, 3):
-                    weight_x(k, to, 1).start()
-            for k in (1, 3, 2):
-                weight_c(k, 0).wait_recv()
 
         rows = jnp.concatenate([acts[k] for k in places], 0)
-        for b in range(NB):
-            sums = jnp.dot(rows, wgu[mod(b - z_hi, 4)], preferred_element_type=F32)
+        for place in (0, 3, 1, 2):
+            if 0 in places and place:
+                weight_c(4 - place, 0).wait_recv()
+            sums = jnp.dot(rows, wgu[place], preferred_element_type=F32)
+            cols = pl.ds(pl.multiple_of(2 * HB * mod(z_hi + place, 4), 2 * HB), 2 * HB)
             for n, k in enumerate(places):
-                terms[k, :, pl.ds(2 * HB * b, 2 * HB)] = sums[ROWS * n:ROWS * (n + 1)]
+                terms[k, :, cols] = sums[ROWS * n:ROWS * (n + 1)]
+        if 0 in places:
+            down_along()
 
     gather(acts, at_y, ag_ssem, ag_rsem, FB, gate_up, weights_begun)
 
@@ -304,8 +314,10 @@
         if 0 in places:
             own[2].wait()
 
-            for k in (1, 3, 2):
-                weight_c(k, 1).wait_recv()
+            @pl.when(c == 0)
+            def _():
+                for k in (1, 3, 2):
+                    weight_c(k, 1).wait_recv()
 
         rows = jnp.concatenate([hid[k] for k in places], 0)
         total = None
@@ -316,10 +328,12 @@
             terms[k] = total[ROWS * n:ROWS * (n + 1)]
 
     def hand_down():
-        for k in (1, 3, 2):
-            for to in (1, 3, 2):
-                weight_x(k, to, 1).wait_recv()
-            weight_c(k, 1).start()
+        @pl.when(c == 1)
+        def _():
+            for k in (1, 3, 2):
+                for to in (1, 3, 2):
+                    weight_x(k, to, 1).wait_recv()
+                weight_c(k, 1).start()
 
     gather(hid, at_z, hg_ssem, hg_rsem, NB * HB, down, hand_down)
 
@@ -351,13 +365,19 @@
         copy.wait_send()
 
     for k in (1, 2, 3):
-        for i in range(3):
+        for i in range(2):
             weight_z(k, i).wait_send()
         for to in (1, 2, 3):
-            for i in range(2):
-                weight_x(k, to, i).wait_send()
-        for i in range(2):
-            weight_c(k, i).wait_send()
+            weight_x(k, to, 0).wait_send()
+        weight_c(k, 0).wait_send()
+
+    @pl.when(c == 1)
+    def _():
+        for k in (1, 2, 3):
+            weight_z(k, 2).wait_send()
+            for to in (1, 2, 3):
+                weight_x(k, to, 1).wait_send()
+            weight_c(k, 1).wait_send()
 
 
 def per_device(q, ck, cv, nk, nv, lengths, residual, gain, gate, up, down):

time: 77.1 us -> 76.8 us (level)
  the two profiles are of different devices: /device:TPU:4 before, /device:TPU:16 now
where the time goes in v5:
time: 76.8 us; the launch traced here: 76.6 us
  Pallas kernels  75.1 us (98%)
  local copies, waits for them, and re-layouts  1.57 us (2%)
    pallas_call x1, Pallas kernels, per_device(): pl.pallas_call(kernel, out_shape=jax.ShapeDtypeStruct((R, QH * HD), BF16)...  75.1 us
    unnamed x1, local copies, waits for them, and re-layouts  1.57 us

profile of v5, /device:TPU:16, one launch (start us, length us, event | category | flops | bytes accessed | tf_op | source)
XLA Modules:
  0.0 76.6 jit_solution(9489681147195873487)
XLA Ops:
  0.0 75.1 %shard_map.109 = bf16[6,8192]{1,0:T(8,128)(2,1)} custom-call(s32[6]{0:T(128)} %len_hbm.1, bf16[6,64,128]{2,1,0:T(8,128)(2,1)} %q_hbm.1, bf16[6,128,512]{2,1,0:T(8,128)(2,1)} %ck_hbm.1, bf16[6,128,512]{2,1,0:T(8,128)(2,1)} %cv_hbm.1, bf16[6,512]{1,0:T(8,128)(2,1)} %nk_hbm.1, bf16[6,512]{1,0:T(8,128)(2,1)} %nv_hbm.1, bf16[6,8192]{1,0:T(8,128)(2,1)} %res_hbm.1, ...), custom_call_target="tpu_custom_call" | custom-call | flops 1400000000 | bytes 5000000 | tf_op jit(solution)/shard_map/pallas_call | solution.py:387
  75.1 1.6 %copy.13 = bf16[6,8192]{1,0:T(8,128)(2,1)} copy(bf16[6,8192]{1,0:T(8,128)(2,1)} %shard_map.109) | data formatting | bytes 196608

commit v6 on v5

--- a/solution.py
+++ b/solution.py
@@ -401,8 +401,8 @@
             pltpu.VMEM((NB, FB, 2 * HB), BF16),
             pltpu.VMEM((NB, HB, FB), BF16),
             pltpu.VMEM((R * QH, L), F32),
-            pltpu.VMEM((R * QH, HD), F32),
-            pltpu.VMEM((R * QH, HD), F32),
+            pltpu.VMEM((8 * QH, HD), F32),
+            pltpu.VMEM((R * QH + 16, HD), F32),
             pltpu.VMEM((N, ROWS, HD), BF16),
             pltpu.VMEM((N, ROWS, HD), BF16),
             pltpu.VMEM((N * ROWS, HD), F32),

time: 76.8 us -> 76.8 us (level)
  no operation moved by 1% of the time
where the time goes in v6:
time: 76.8 us; the launch traced here: 76.6 us
  Pallas kernels  75.1 us (98%)
  local copies, waits for them, and re-layouts  1.57 us (2%)
    pallas_call x1, Pallas kernels, per_device(): pl.pallas_call(kernel, out_shape=jax.ShapeDtypeStruct((R, QH * HD), BF16)...  75.1 us
    unnamed x1, local copies, waits for them, and re-layouts  1.57 us

profile of v6, /device:TPU:16, one launch (start us, length us, event | category | flops | bytes accessed | tf_op | source)
XLA Modules:
  0.0 76.6 jit_solution(3709121223899017943)
XLA Ops:
  0.0 75.1 %shard_map.109 = bf16[6,8192]{1,0:T(8,128)(2,1)} custom-call(s32[6]{0:T(128)} %len_hbm.1, bf16[6,64,128]{2,1,0:T(8,128)(2,1)} %q_hbm.1, bf16[6,128,512]{2,1,0:T(8,128)(2,1)} %ck_hbm.1, bf16[6,128,512]{2,1,0:T(8,128)(2,1)} %cv_hbm.1, bf16[6,512]{1,0:T(8,128)(2,1)} %nk_hbm.1, bf16[6,512]{1,0:T(8,128)(2,1)} %nv_hbm.1, bf16[6,8192]{1,0:T(8,128)(2,1)} %res_hbm.1, ...), custom_call_target="tpu_custom_call" | custom-call | flops 1400000000 | bytes 5000000 | tf_op jit(solution)/shard_map/pallas_call | solution.py:387
  75.1 1.6 %copy.13 = bf16[6,8192]{1,0:T(8,128)(2,1)} copy(bf16[6,8192]{1,0:T(8,128)(2,1)} %shard_map.109) | data formatting | bytes 196608
